TPU v7x, 128 devices: a whole 4x4x4 slice. The times are simulated.
128 devices in a mesh: gx: 32 (over y, z_hi, x), gy: 4 (over z_lo, core).
Axes of the slice: x: 4, y: 4, z: 4 (z_hi: 2, z_lo: 2; z = z_hi * 2 + z_lo), core: 2. Of those that a mesh axis runs over, the one named last changes fastest.
Arguments:
- occupied: bfloat16 [256, 8, 32768], P(('gx', 'gy')), may hold values from -6 to 6
- virtual: bfloat16 [256, 8, 32768], P(('gx', 'gy')), may hold values from -6 to 6
- trials: bfloat16 [256, 4, 8, 8], P(('gx', 'gy')), may hold values from -1 to 1
- anchor_x: int32 [256], P(('gx', 'gy')), may hold values from 0 to 7
- anchor_y: int32 [256], P(('gx', 'gy')), may hold values from 0 to 127
- anchor_z: int32 [256], P(('gx', 'gy')), may hold values from 0 to 96
Outputs:
- potential: float32 [4, 256, 512, 128], P(None, 'gx', 'gy')
- coupling: float32 [256, 4, 8, 8], P(('gx', 'gy'))
All inputs are finite; a program needn't handle non-finite values.
Results may differ from a plain program's by a relative error of at most 0.00051.
Values sent between devices are 32-bit elements; how exact they have to be, the bound alone decides.
A program may use at most 192 MiB of HBM per device.

v0:
```python
import jax
import jax.numpy as jnp
from jax import lax
from jax.sharding import PartitionSpec as P

BOX = 32
TRIALS = 4
LEVELS = 3
CX = 8
CY = 128
NZ = 128


SCREEN = 0.05
DAMPING = 2.0 / 3.0


def extended_2(x, sides, width):
    for axis, dim in sides:
        size, length = (lax.axis_size(axis), x.shape[dim])
        up = [(i, (i + 1) % size) for i in range(size)]
        down = [(j, i) for i, j in up]
        last = lax.slice_in_dim(x, length - width, length, axis=dim)
        first = lax.slice_in_dim(x, 0, width, axis=dim)
        before = lax.ppermute(last, axis, up)
        after = lax.ppermute(first, axis, down)
        x = jnp.concatenate([before, x, after], axis=dim)
    return x


def passed_along(x, axis, by):
    length = lax.axis_size(axis)
    return lax.ppermute(x, axis, [(i, (i + by) % length) for i in range(length)])


def hartley(count):
    index = jnp.arange(count, dtype=jnp.int32)
    product = index[:, None] * index[None, :] % count
    angle = 2.0 * jnp.pi / count * product.astype(jnp.float32)
    return (jnp.cos(angle) + jnp.sin(angle)) / jnp.sqrt(jnp.float32(count))


def eigen_line(count, spacing):
    index = jnp.arange(count, dtype=jnp.int32).astype(jnp.float32)
    return (2.0 - 2.0 * jnp.cos(2.0 * jnp.pi / count * index)) / (spacing * spacing)


def transform_all(field, table_x, table_y, table_z):
    high = lax.Precision.HIGHEST
    field = jnp.einsum("txyz,xa->tayz", field, table_x, precision=high)
    field = jnp.einsum("tayz,yb->tabz", field, table_y, precision=high)
    return jnp.einsum("tabz,zc->tabc", field, table_z, precision=high)


def eigen_grid(size_x, size_y, size_z, spacing):
    return (
        SCREEN * SCREEN
        + eigen_line(size_x, spacing)[:, None, None]
        + eigen_line(size_y, spacing)[None, :, None]
        + eigen_line(size_z, spacing)[None, None, :]
    )


def coarse_solve(source, spacing):
    trial_count, cells_x, cells_y, cells_z = source.shape
    slabs_x = lax.axis_size("gx")
    tiles_y = lax.axis_size("gy")
    size_x = slabs_x * cells_x
    size_y = tiles_y * cells_y
    row_x = lax.axis_index("gx") * cells_x
    row_y = lax.axis_index("gy") * cells_y
    eigen_values = eigen_grid(size_x, size_y, cells_z, spacing)
    table_z = hartley(cells_z)
    flat = source.reshape(1, trial_count, cells_x * cells_y * cells_z)
    everything = lax.all_gather(flat, ("gx", "gy"), axis=0, tiled=True)
    whole = everything.reshape(slabs_x, tiles_y, trial_count, cells_x, cells_y, cells_z)
    whole = whole.transpose(2, 0, 3, 1, 4, 5).reshape(trial_count, size_x, size_y, cells_z)
    table_x, table_y = (hartley(size_x), hartley(size_y))
    spectrum = transform_all(whole, table_x, table_y, table_z)
    solved = transform_all(spectrum / eigen_values, table_x, table_y, table_z)
    return lax.dynamic_slice(solved, (jnp.int32(0), row_x, row_y, jnp.int32(0)), source.shape)


def operate(field, spacing):
    padded = extended_2(field, (("gx", 1), ("gy", 2)), 1)
    beside = padded[:, 2:, 1:-1] + padded[:, :-2, 1:-1]
    beside = beside + padded[:, 1:-1, 2:] + padded[:, 1:-1, :-2]
    beside = beside + jnp.roll(field, -1, 3) + jnp.roll(field, 1, 3)
    return (6.0 / spacing**2 + SCREEN**2) * field - beside / spacing**2


def restrict(field):
    trial_count, size_x, size_y, size_z = field.shape
    blocks = field.reshape(trial_count, size_x // 2, 2, size_y // 2, 2, size_z // 2, 2)
    return blocks.mean(axis=(2, 4, 6))


def prolong(field):
    return jnp.repeat(jnp.repeat(jnp.repeat(field, 2, 1), 2, 2), 2, 3)


def vcycle(source, depth_level):
    spacing = 2.0**depth_level
    if depth_level == LEVELS:
        return coarse_solve(source, spacing)
    center = 6.0 / spacing**2 + SCREEN**2
    first = DAMPING * source / center
    residue = source - operate(first, spacing)
    second = first + prolong(vcycle(restrict(residue), depth_level + 1))
    return second + DAMPING * (source - operate(second, spacing)) / center


def per_device(occupied, virtual, trials, anchor_x, anchor_y, anchor_z):
    box_count = occupied.shape[0]
    slab_count = (BOX + CX - 1) // CX
    zero = jnp.int32(0)
    extended = jnp.zeros((TRIALS, CX * (1 + slab_count), CY + BOX, NZ), jnp.float32)
    for box_index in range(box_count):
        mixture = jnp.einsum(
            "tia,ar->tir", trials[box_index], virtual[box_index], preferred_element_type=jnp.float32
        )
        box_density = jnp.sum(occupied[box_index][None] * mixture, axis=1)
        spot = (zero, anchor_x[box_index], anchor_y[box_index], anchor_z[box_index])
        block = lax.dynamic_slice(extended, spot, (TRIALS, BOX, BOX, BOX))
        block = block + box_density.reshape(TRIALS, BOX, BOX, BOX)
        extended = lax.dynamic_update_slice(extended, block, spot)
    upper_rim = passed_along(extended[:, :, CY:], "gy", 1)
    folded = extended[:, :, :CY].at[:, :, :BOX].add(upper_rim)
    owned = folded[:, :CX]
    pieces = [
        folded[:, CX * (slab_index + 1) : CX * (slab_index + 2)] for slab_index in range(slab_count)
    ]
    for slab_index in range(slab_count):
        owned = owned + passed_along(pieces[slab_index], "gx", slab_index + 1)
    potential = vcycle(owned, 0)
    parts = [potential]
    for slab_index in range(slab_count):
        parts.append(passed_along(potential, "gx", -(slab_index + 1)))
    widened = jnp.concatenate(parts, axis=1)
    margin = passed_along(widened[:, :, :BOX], "gy", -1)
    padded = jnp.concatenate([widened, margin], axis=2)
    scale = float(BOX) ** (-1.5)
    results = []
    for box_index in range(box_count):
        spot = (zero, anchor_x[box_index], anchor_y[box_index], anchor_z[box_index])
        window = lax.dynamic_slice(padded, spot, (TRIALS, BOX, BOX, BOX)).reshape(
            TRIALS, BOX * BOX * BOX
        )
        weighted = (occupied[box_index][None] * window[:, None]).astype(jnp.bfloat16)
        product = jnp.einsum(
            "tir,ar->tia", weighted, virtual[box_index], preferred_element_type=jnp.float32
        )
        results.append(scale * product)
    coupling = jnp.stack(results, axis=0)
    return (potential, coupling)


def solution(mesh):
    placed = (
        P(("gx", "gy"), None, None),
        P(("gx", "gy"), None, None),
        P(("gx", "gy"), None, None, None),
        P(("gx", "gy")),
        P(("gx", "gy")),
        P(("gx", "gy")),
    )
    return jax.shard_map(
        per_device,
        mesh=mesh,
        in_specs=placed,
        out_specs=(P(None, "gx", "gy", None), P(("gx", "gy"), None, None, None)),
        check_vma=False,
    )
```

profile of v0, /device:TPU:7, one launch (start us, length us, event | category | flops | bytes accessed | tf_op | source)
XLA Modules:
  0.0 1057.6 jit_solution(10314748241472326665)
XLA Ops:
  24.7 6.4 broadcast_in_dim.44
  31.2 49.6 %dynamic_update_slice.6 = f32[4,40,160,128]{3,2,1,0:T(8,128)} dynamic-update-slice(f32[4,40,160,128]{3,2,1,0:T(8,128)} %broadcast_in_dim.44, f32[4,32,32,32]{3,2,1,0:T(8,128)} %reshape.166, s32[]{:T(128)} %constant.134.clone.1, s32[]{:T(128)S(6)} %select_n.58, s32[]{:T(128)S(6)} %select_n.59, s32[]{:T(128)S(6)} %select_n.60) | dynamic-update-slice | bytes 1048580 | tf_op jit(solution)/shard_map/dynamic_update_slice | solution.py:126
  84.5 49.6 %dynamic_update_slice.7 = f32[4,40,160,128]{3,2,1,0:T(8,128)} dynamic-update-slice(f32[4,40,160,128]{3,2,1,0:T(8,128)} %dynamic_update_slice.6, f32[4,32,32,32]{3,2,1,0:T(8,128)} %dynamic-slice_add_fusion, s32[]{:T(128)} %constant.134.clone.1, s32[]{:T(128)S(6)} %select_n.61, s32[]{:T(128)S(6)} %select_n.62, s32[]{:T(128)S(6)} %select_n.63) | dynamic-update-slice | bytes 1048580 | tf_op jit(solution)/shard_map/dynamic_update_slice | solution.py:126
  143.3 23.7 %collective-permute-done = f32[4,40,32,128]{3,2,1,0:T(8,128)} collective-permute-done((f32[4,40,32,128]{3,2,1,0:T(8,128)S(1)}, f32[4,40,32,128]{3,2,1,0:T(8,128)}, u32[]{:S(2)}, u32[]{:S(2)}) %collective-permute-start) | collective-permute-done | bytes 2621472 | tf_op jit(solution)/shard_map/ppermute | solution.py:33
  186.9 38.5 %collective-permute-done.1 = f32[4,8,128,128]{3,2,1,0:T(8,128)S(1)} collective-permute-done((f32[4,8,128,128]{3,2,1,0:T(8,128)}, f32[4,8,128,128]{3,2,1,0:T(8,128)S(1)}, u32[]{:S(2)}, u32[]{:S(2)}) %collective-permute-start.1) | collective-permute-done | bytes 2097184 | tf_op jit(solution)/shard_map/ppermute | solution.py:33
  227.8 46.7 %collective-permute-done.3 = f32[4,8,128,128]{3,2,1,0:T(8,128)} collective-permute-done((f32[4,8,128,128]{3,2,1,0:T(8,128)}, f32[4,8,128,128]{3,2,1,0:T(8,128)}, u32[]{:S(2)}, u32[]{:S(2)}) %collective-permute-start.3) | collective-permute-done | bytes 2097184 | tf_op jit(solution)/shard_map/ppermute | solution.py:33
  279.9 16.7 %collective-permute-start.5 = (f32[4,1,128,128]{3,2,1,0:T(8,128)S(1)}, f32[4,1,128,128]{3,2,1,0:T(8,128)S(1)}, u32[]{:S(2)}, u32[]{:S(2)}) collective-permute-start(f32[4,1,128,128]{3,2,1,0:T(8,128)S(1)} %get-tuple-element.41), channel_id=1, source_target_pairs={{4,0},{8,4},{12,8},{16,12},{20,16},{24,20},{28,24},{32,28},{36,32}... | collective-permute-start | bytes 786440 | tf_op jit(solution)/shard_map/ppermute | solution.py:26
  296.6 75.4 %collective-permute-start.6 = (f32[4,1,128,128]{3,2,1,0:T(8,128)S(1)}, f32[4,1,128,128]{3,2,1,0:T(8,128)S(1)}, u32[]{:S(2)}, u32[]{:S(2)}) collective-permute-start(f32[4,1,128,128]{3,2,1,0:T(8,128)S(1)} %get-tuple-element.40), channel_id=1, source_target_pairs={{0,4},{4,8},{8,12},{12,16},{16,20},{20,24},{24,28},{28,32},{32,36}... | collective-permute-start | bytes 786440 | tf_op jit(solution)/shard_map/ppermute | solution.py:25
  385.0 33.8 %copy.304 = f32[4,8,128,128]{0,3,2,1:T(8,128)} copy(f32[4,8,128,128]{3,2,1,0:T(8,128)} %fusion.18) | data formatting | bytes 4194304 | tf_op jit(solution)/shard_map/sub | solution.py:108
  418.8 46.6 %reduce_sum.54 = f32[4,4,64,64]{0,3,2,1:T(8,128)} reduce(f32[4,4,2,64,2,64,2]{0,6,5,4,3,2,1:T(2,128)} %bitcast.14, f32[]{:T(128)} %constant.133.clone.1), dimensions={2,4,6}, to_apply=%region_2.0 | reduce | flops 458752 | bytes 2359300 | tf_op jit(solution)/shard_map/reduce_sum | solution.py:95
  465.4 5.5 copy.305
  477.8 5.5 collective-permute-done.9
  493.3 10.0 reduce_sum.55
  517.4 171.4 %all_gather.3 = f32[128,4,256]{2,1,0:T(4,128)S(1)} all-gather(f32[1,4,256]{2,1,0:T(4,128)S(1)} %copy.317), channel_id=1, replica_groups=mesh['gx'=32,'gy'=4] {'gx','gy'}, dimensions={0}, use_global_device_ids=true | all-gather | bytes 528384 | tf_op jit(solution)/shard_map/all_gather | solution.py:75
  703.4 6.9 fusion.101
  710.6 5.8 collective-permute-start.17
  717.8 6.4 collective-permute-done.18
  730.5 5.8 collective-permute-start.21
  756.1 7.2 collective-permute-start.25
  776.8 95.5 %collective-permute-start.29 = (f32[4,8,128,128]{3,2,1,0:T(8,128)S(1)}, f32[4,8,128,128]{3,2,1,0:T(8,128)S(1)}, u32[]{:S(2)}, u32[]{:S(2)}) collective-permute-start(f32[4,8,128,128]{3,2,1,0:T(8,128)S(1)} %get-tuple-element.17), channel_id=1, source_target_pairs={{0,124},{4,0},{8,4},{12,8},{16,12},{20,16},{24,20},{28,24},{32,28}... | collective-permute-start | bytes 6291464 | tf_op jit(solution)/shard_map/ppermute | solution.py:33
  872.4 44.5 %collective-permute-done.29 = f32[4,8,128,128]{3,2,1,0:T(8,128)S(1)} collective-permute-done((f32[4,8,128,128]{3,2,1,0:T(8,128)S(1)}, f32[4,8,128,128]{3,2,1,0:T(8,128)S(1)}, u32[]{:S(2)}, u32[]{:S(2)}) %collective-permute-start.29) | collective-permute-done | bytes 2097184 | tf_op jit(solution)/shard_map/ppermute | solution.py:33
  917.0 44.8 %collective-permute-done.30 = f32[4,8,128,128]{3,2,1,0:T(8,128)S(1)} collective-permute-done((f32[4,8,128,128]{3,2,1,0:T(8,128)S(1)}, f32[4,8,128,128]{3,2,1,0:T(8,128)S(1)}, u32[]{:S(2)}, u32[]{:S(2)}) %collective-permute-start.30) | collective-permute-done | bytes 2097184 | tf_op jit(solution)/shard_map/ppermute | solution.py:33
  966.3 45.9 %collective-permute-done.32 = f32[4,8,128,128]{3,2,1,0:T(8,128)S(1)} collective-permute-done((f32[4,8,128,128]{3,2,1,0:T(8,128)S(1)}, f32[4,8,128,128]{3,2,1,0:T(8,128)S(1)}, u32[]{:S(2)}, u32[]{:S(2)}) %collective-permute-start.32) | collective-permute-done | bytes 2097184 | tf_op jit(solution)/shard_map/ppermute | solution.py:33
  1013.2 30.6 %collective-permute-done.33 = f32[4,40,32,128]{3,2,1,0:T(8,128)S(1)} collective-permute-done((f32[4,40,32,128]{3,2,1,0:T(8,128)S(1)}, f32[4,40,32,128]{3,2,1,0:T(8,128)S(1)}, u32[]{:S(2)}, u32[]{:S(2)}) %collective-permute-start.33) | collective-permute-done | bytes 2621472 | tf_op jit(solution)/shard_map/ppermute | solution.py:33
  (174 shorter events, 171.9 us)
Async XLA Ops:
  136.2 30.9 %collective-permute-start = (f32[4,40,32,128]{3,2,1,0:T(8,128)S(1)}, f32[4,40,32,128]{3,2,1,0:T(8,128)}, u32[]{:S(2)}, u32[]{:S(2)}) collective-permute-start(f32[4,40,32,128]{3,2,1,0:T(8,128)S(1)} %slice.447), channel_id=1, source_target_pairs={{0,1},{1,2},{2,3},{3,0},{4,5},{5,6},{6,7},{7,4},{8,9},{9,10},{10,1... | collective-permute-start | bytes 7864328 | tf_op jit(solution)/shard_map/ppermute | solution.py:33
  177.0 48.4 %collective-permute-start.1 = (f32[4,8,128,128]{3,2,1,0:T(8,128)}, f32[4,8,128,128]{3,2,1,0:T(8,128)S(1)}, u32[]{:S(2)}, u32[]{:S(2)}) collective-permute-start(f32[4,8,128,128]{3,2,1,0:T(8,128)} %get-tuple-element.22), channel_id=1, source_target_pairs={{0,4},{4,8},{8,12},{12,16},{16,20},{20,24},{24,28},{28,32},{32,36}... | collective-permute-start | bytes 6291464 | tf_op jit(solution)/shard_map/ppermute | solution.py:33
  180.2 47.6 %collective-permute-start.2 = (f32[4,8,128,128]{3,2,1,0:T(8,128)}, f32[4,8,128,128]{3,2,1,0:T(8,128)}, u32[]{:S(2)}, u32[]{:S(2)}) collective-permute-start(f32[4,8,128,128]{3,2,1,0:T(8,128)} %get-tuple-element.25), channel_id=1, source_target_pairs={{0,8},{4,12},{8,16},{12,20},{16,24},{20,28},{24,32},{28,36},{32,40... | collective-permute-start | bytes 6291464 | tf_op jit(solution)/shard_map/ppermute | solution.py:33
  182.3 92.2 %collective-permute-start.3 = (f32[4,8,128,128]{3,2,1,0:T(8,128)}, f32[4,8,128,128]{3,2,1,0:T(8,128)}, u32[]{:S(2)}, u32[]{:S(2)}) collective-permute-start(f32[4,8,128,128]{3,2,1,0:T(8,128)} %get-tuple-element.24), channel_id=1, source_target_pairs={{0,12},{4,16},{8,20},{12,24},{16,28},{20,32},{24,36},{28,40},{32,4... | collective-permute-start | bytes 6291464 | tf_op jit(solution)/shard_map/ppermute | solution.py:33
  182.4 92.1 %collective-permute-start.4 = (f32[4,8,128,128]{3,2,1,0:T(8,128)}, f32[4,8,128,128]{3,2,1,0:T(8,128)}, u32[]{:S(2)}, u32[]{:S(2)}) collective-permute-start(f32[4,8,128,128]{3,2,1,0:T(8,128)} %get-tuple-element.23), channel_id=1, source_target_pairs={{0,16},{4,20},{8,24},{12,28},{16,32},{20,36},{24,40},{28,44},{32,4... | collective-permute-start | bytes 6291464 | tf_op jit(solution)/shard_map/ppermute | solution.py:33
  279.9 98.3 %collective-permute-start.5 = (f32[4,1,128,128]{3,2,1,0:T(8,128)S(1)}, f32[4,1,128,128]{3,2,1,0:T(8,128)S(1)}, u32[]{:S(2)}, u32[]{:S(2)}) collective-permute-start(f32[4,1,128,128]{3,2,1,0:T(8,128)S(1)} %get-tuple-element.41), channel_id=1, source_target_pairs={{4,0},{8,4},{12,8},{16,12},{20,16},{24,20},{28,24},{32,28},{36,32}... | collective-permute-start | bytes 786440 | tf_op jit(solution)/shard_map/ppermute | solution.py:26
  296.6 81.6 %collective-permute-start.6 = (f32[4,1,128,128]{3,2,1,0:T(8,128)S(1)}, f32[4,1,128,128]{3,2,1,0:T(8,128)S(1)}, u32[]{:S(2)}, u32[]{:S(2)}) collective-permute-start(f32[4,1,128,128]{3,2,1,0:T(8,128)S(1)} %get-tuple-element.40), channel_id=1, source_target_pairs={{0,4},{4,8},{8,12},{12,16},{16,20},{20,24},{24,28},{28,32},{32,36}... | collective-permute-start | bytes 786440 | tf_op jit(solution)/shard_map/ppermute | solution.py:25
  471.0 6.9 collective-permute-start.10
  475.9 7.4 collective-permute-start.9
  505.1 6.8 collective-permute-start.13
  505.2 6.7 collective-permute-start.14
  511.9 4.5 collective-permute-start.15
  710.6 7.2 collective-permute-start.17
  716.4 7.8 collective-permute-start.18
  730.5 7.7 collective-permute-start.21
  736.3 4.0 collective-permute-start.22
  740.3 4.5 collective-permute-start.23
  756.1 12.5 %collective-permute-start.25 = (f32[4,1,128,128]{3,2,1,0:T(8,128)S(1)}, f32[4,1,128,128]{3,2,1,0:T(8,128)S(1)}, u32[]{:S(2)}, u32[]{:S(2)}) collective-permute-start(f32[4,1,128,128]{3,2,1,0:T(8,128)S(1)} %get-tuple-element.31), channel_id=1, source_target_pairs={{4,0},{8,4},{12,8},{16,12},{20,16},{24,20},{28,24},{32,28},{36,32}... | collective-permute-start | bytes 786440 | tf_op jit(solution)/shard_map/ppermute | solution.py:26
  763.3 7.8 collective-permute-start.26
  776.8 140.1 %collective-permute-start.29 = (f32[4,8,128,128]{3,2,1,0:T(8,128)S(1)}, f32[4,8,128,128]{3,2,1,0:T(8,128)S(1)}, u32[]{:S(2)}, u32[]{:S(2)}) collective-permute-start(f32[4,8,128,128]{3,2,1,0:T(8,128)S(1)} %get-tuple-element.17), channel_id=1, source_target_pairs={{0,124},{4,0},{8,4},{12,8},{16,12},{20,16},{24,20},{28,24},{32,28}... | collective-permute-start | bytes 6291464 | tf_op jit(solution)/shard_map/ppermute | solution.py:33
  872.4 89.5 %collective-permute-start.30 = (f32[4,8,128,128]{3,2,1,0:T(8,128)S(1)}, f32[4,8,128,128]{3,2,1,0:T(8,128)S(1)}, u32[]{:S(2)}, u32[]{:S(2)}) collective-permute-start(f32[4,8,128,128]{3,2,1,0:T(8,128)S(1)} %get-tuple-element.17), channel_id=1, source_target_pairs={{0,120},{4,124},{8,0},{12,4},{16,8},{20,12},{24,16},{28,20},{32,24... | collective-permute-start | bytes 6291464 | tf_op jit(solution)/shard_map/ppermute | solution.py:33
  872.4 93.8 %collective-permute-start.31 = (f32[4,8,128,128]{3,2,1,0:T(8,128)S(1)}, f32[4,8,128,128]{3,2,1,0:T(8,128)S(1)}, u32[]{:S(2)}, u32[]{:S(2)}) collective-permute-start(f32[4,8,128,128]{3,2,1,0:T(8,128)S(1)} %get-tuple-element.17), channel_id=1, source_target_pairs={{0,116},{4,120},{8,124},{12,0},{16,4},{20,8},{24,12},{28,16},{32,2... | collective-permute-start | bytes 6291464 | tf_op jit(solution)/shard_map/ppermute | solution.py:33
  872.4 139.8 %collective-permute-start.32 = (f32[4,8,128,128]{3,2,1,0:T(8,128)S(1)}, f32[4,8,128,128]{3,2,1,0:T(8,128)S(1)}, u32[]{:S(2)}, u32[]{:S(2)}) collective-permute-start(f32[4,8,128,128]{3,2,1,0:T(8,128)S(1)} %get-tuple-element.17), channel_id=1, source_target_pairs={{0,112},{4,116},{8,120},{12,124},{16,0},{20,4},{24,8},{28,12},{32,... | collective-permute-start | bytes 6291464 | tf_op jit(solution)/shard_map/ppermute | solution.py:33
  1012.6 31.1 %collective-permute-start.33 = (f32[4,40,32,128]{3,2,1,0:T(8,128)S(1)}, f32[4,40,32,128]{3,2,1,0:T(8,128)S(1)}, u32[]{:S(2)}, u32[]{:S(2)}) collective-permute-start(f32[4,40,32,128]{3,2,1,0:T(8,128)S(1)} %slice.489), channel_id=1, source_target_pairs={{0,3},{1,0},{2,1},{3,2},{4,7},{5,4},{6,5},{7,6},{8,11},{9,8},{10,9... | collective-permute-start | bytes 7864328 | tf_op jit(solution)/shard_map/ppermute | solution.py:33
  (19 other events, 261.7 us)
where the time goes:
time: 1070 us; the launch traced here: 1060 us
  waiting for transfers between devices  319 us (30%)
  starting transfers between devices  244 us (23%)
  local copies, waits for them, and re-layouts  202 us (19%)
  blocking collectives  171 us (16%)
  other arithmetic  85.1 us (8%)
  matrix products  22.9 us (2%)
  between operations  12.8 us (1%)
    ppermute x10, waiting for transfers between devices, passed_along(): lax.ppermute(x, axis, [(i, (i + by) % length) for i in range(length)])  281 us
    all_gather x1, blocking collectives, coarse_solve(): everything = lax.all_gather(flat, ('gx', 'gy'), axis=0, tiled=True)  171 us
    ppermute x10, starting transfers between devices, passed_along(): lax.ppermute(x, axis, [(i, (i + by) % length) for i in range(length)])  107 us
    dynamic_update_slice x2, local copies, waits for them, and re-layouts, per_device(): extended = lax.dynamic_update_slice(extended, block, spot)  99.3 us
    ppermute x12, starting transfers between devices, extended_2(): before = lax.ppermute(last, axis, up)  89 us
    reduce_sum x4, other arithmetic, restrict(): return blocks.mean(axis=(2, 4, 6))  57.1 us
    ppermute x12, starting transfers between devices, extended_2(): after = lax.ppermute(first, axis, down)  47.7 us
    sub x2, local copies, waits for them, and re-layouts, vcycle(): residue = source - operate(first, spacing)  38.8 us
  transfers between devices with their start and end apart: 34, of which 26 were waited for; matrix products, arithmetic and copies ran while one was open for 1% of the time, Pallas kernels for 0%

commit v1 on v0

v1 whole, which is shorter than its diff:
```python
import functools

import jax
import jax.numpy as jnp
import numpy as np
from jax import lax
from jax.experimental import pallas as pl
from jax.experimental.pallas import tpu as pltpu
from jax.sharding import PartitionSpec as P

BOX = 32
TRIALS = 4
CX = 8
CY = 128
NZ = 128
SCREEN = 0.05
DAMPING = 2.0 / 3.0
MESH = pl.DeviceIdType.MESH
F32 = jnp.float32
BF16 = jnp.bfloat16
HIGH = lax.Precision.HIGHEST
VMEM = pl.BlockSpec(memory_space=pltpu.VMEM)
SMEM = pl.BlockSpec(memory_space=pltpu.SMEM)
ANY = pl.BlockSpec(memory_space=pl.ANY)


def center_of(level):
    spacing = 2.0**level
    return 6.0 / spacing**2 + SCREEN**2


def split2(x):
    hi = x.astype(BF16)
    lo = (x - hi.astype(F32)).astype(BF16)
    return hi, lo


def dot(a, b):
    return jnp.dot(a, b, preferred_element_type=F32)


def dot_right(x, w):
    hi, lo = split2(x)
    return dot(hi, w) + dot(lo, w)


def dot_left(w, x):
    hi, lo = split2(x)
    return dot(w, hi) + dot(w, lo)


def dot_high(a, b):
    return jnp.dot(a, b, preferred_element_type=F32, precision=HIGH)


def z_beside(x, n):
    if n == 128:
        return pltpu.roll(x, 1, 1) + pltpu.roll(x, 127, 1)
    lane = lax.broadcasted_iota(jnp.int32, x.shape, 1) % n
    below = jnp.where(lane == 0, pltpu.roll(x, 129 - n, 1), pltpu.roll(x, 1, 1))
    above = jnp.where(lane == n - 1, pltpu.roll(x, n - 1, 1), pltpu.roll(x, 127, 1))
    return below + above


def hartley_np(count):
    index = np.arange(count)
    angle = 2.0 * np.pi / count * ((index[:, None] * index[None, :]) % count)
    return (np.cos(angle) + np.sin(angle)) / np.sqrt(count)


def eigen_np(count, spacing):
    return (2.0 - 2.0 * np.cos(2.0 * np.pi / count * np.arange(count))) / (spacing * spacing)


@functools.lru_cache(None)
def tables(slabs, tiles):
    out = {}
    r0 = np.zeros((2, 128, 2, 64))
    r1 = np.zeros((2, 2, 64, 4, 32))
    p1 = np.zeros((2, 4, 32, 2, 64))
    p0 = np.zeros((2, 64, 2, 128))
    for t in range(2):
        for z in range(128):
            r0[t, z, t, z // 2] = 0.125
            p0[t, z // 2, t, z] = 1.0
        for z in range(64):
            for p in range(2):
                r1[p, t, z, 2 * p + t, z // 2] = 0.125
                p1[p, 2 * p + t, z // 2, t, z] = 1.0
    out["r0"] = r0.reshape(256, 128)
    out["r1"] = r1.reshape(2, 128, 128)
    out["p1"] = p1.reshape(2, 128, 128)
    out["p0"] = p0.reshape(128, 256)
    hz = hartley_np(16)
    mean_z = np.zeros((32, 16))
    mean_z[np.arange(32), np.arange(32) // 2] = 1.0
    fz = np.zeros((4, 32, 128))
    bz = np.zeros((128, 4, 32))
    for t in range(4):
        fz[t, :, t * 16 : t * 16 + 16] = 0.125 * mean_z @ hz
        bz[t * 16 : t * 16 + 16, t, :] = hz @ mean_z.T
    out["fz"] = fz.reshape(128, 128)
    out["bz"] = bz.reshape(128, 128)
    size_y = 16 * tiles
    hy = hartley_np(size_y)
    mean_y = np.zeros((16, 32))
    mean_y[np.arange(32) // 2, np.arange(32)] = 1.0
    fy = np.zeros((tiles, size_y, 128))
    by = np.zeros((tiles, 48, 128))
    for q in range(tiles):
        fy[q, :, :32] = hy[:, q * 16 : q * 16 + 16] @ mean_y
        for y in range(-2, 34):
            by[q, 8 + y, :size_y] = hy[(q * 16 + y // 2) % size_y]
    out["fy"] = fy
    out["by"] = by
    out["kx"] = np.kron(hartley_np(slabs), np.eye(8))
    lam_x, lam_y, lam_z = eigen_np(slabs, 8.0), eigen_np(size_y, 8.0), eigen_np(16, 8.0)
    inv = np.zeros((tiles, slabs, 8, 2, 4, 16))
    for q in range(tiles):
        ky = lam_y[q * 16 : q * 16 + 16].reshape(2, 8)
        total = (
            SCREEN * SCREEN
            + lam_x[:, None, None, None, None]
            + ky.T[None, :, :, None, None]
            + lam_z[None, None, None, None, :]
        )
        inv[q] = np.broadcast_to(1.0 / total, (slabs, 8, 2, 4, 16))
    out["inv"] = inv.reshape(tiles, slabs * 8, 128)
    return out


def density_kernel(ax_ref, occ_ref, vir_ref, mix_ref, out_ref):
    out_ref[...] = jnp.zeros_like(out_ref)
    for b in range(2):
        weights = mix_ref[b]

        def step(s, carry, b=b, weights=weights):
            rows = pl.ds(pl.multiple_of(s * 16, 16), 16)
            vir = vir_ref[b, :, rows, :].astype(F32)
            occ = occ_ref[b, :, rows, :].astype(F32)
            parts = [vir[:, 8 * h : 8 * h + 8].reshape(64, 128) for h in range(2)]
            mixed = dot(weights, jnp.concatenate(parts, axis=1).astype(BF16))
            mixed = mixed.reshape(8, 4, 8, 256)
            for h in range(2):
                dens = jnp.sum(occ[:, None, 8 * h : 8 * h + 8] * mixed[..., 128 * h : 128 * h + 128], axis=0)
                out_ref[ax_ref[b] + 2 * s + h, b] = dens
            return carry

        lax.fori_loop(0, 16, step, 0)


def deposit_kernel(src_ref, anc_ref, got_ref, ganc_ref, send, recv):
    gx, gy = lax.axis_index("gx"), lax.axis_index("gy")
    n = lax.axis_size("gx")
    targets = [1, 2, 3, 4, -1]
    barrier = pltpu.get_barrier_semaphore()
    for k in targets:
        pl.semaphore_signal(barrier, inc=1, device_id=(lax.rem(gx - k + n, n), gy), device_id_type=MESH)
    pl.semaphore_wait(barrier, 5)
    pieces = [(7, 10, 0), (15, 10, 0), (23, 10, 0), (31, 8, 0), (0, 1, 9)]
    copies = []
    for s, k in enumerate(targets):
        first, count, to = pieces[s]
        where = (lax.rem(gx + k + n, n), gy)
        copies.append(
            pltpu.make_async_remote_copy(
                src_ref=anc_ref,
                dst_ref=ganc_ref.at[s],
                send_sem=send.at[5 + s],
                recv_sem=recv.at[5 + s],
                device_id=where,
                device_id_type=MESH,
            )
        )
        copies.append(
            pltpu.make_async_remote_copy(
                src_ref=src_ref.at[pl.ds(first, count)],
                dst_ref=got_ref.at[s, pl.ds(to, count)],
                send_sem=send.at[s],
                recv_sem=recv.at[s],
                device_id=where,
                device_id_type=MESH,
            )
        )
    for c in copies:
        c.start()
    for c in copies:
        c.wait()


def box_anchors(anc_ref, ganc_ref, sources):
    pairs = []
    for s in sources:
        for b in range(2):
            if s < 0:
                pairs.append((anc_ref[0, b], anc_ref[0, 2 + b]))
            else:
                pairs.append((ganc_ref[s, 0, b], ganc_ref[s, 0, 2 + b]))
    return pairs


def select_rows(pairs):
    row = lax.broadcasted_iota(jnp.int32, (160, 320), 0)
    col = lax.broadcasted_iota(jnp.int32, (160, 320), 1)
    want = 4 * (col % 8) + (col // 8) % 4
    box = col // 32
    for k, (ay, _) in enumerate(pairs):
        want = want + jnp.where(box == k, ay, 0)
    return jnp.where(row == want, 1.0, 0.0).astype(BF16)


def accumulate_kernel(anc_ref, ganc_ref, own_ref, got_ref, out_ref, sel_ref):
    usual = box_anchors(anc_ref, ganc_ref, [-1, 0, 1, 2, 3])
    last = box_anchors(anc_ref, ganc_ref, [-1, 0, 1, 2, 4])
    sel_ref[0] = select_rows(usual)
    sel_ref[1] = select_rows(last)
    lane = lax.broadcasted_iota(jnp.int32, (8, 128), 1)
    blank = jnp.zeros((8, 128), F32)

    def plane(e, which, own, got, edge):
        pairs = last if edge else usual
        loads = []
        for s in range(5):
            for b in range(2):
                if s == 0:
                    loads.append((lambda t, b=b: own_ref[e - 1, b, t]) if own else None)
                elif s == 4 and edge:
                    loads.append(lambda t, b=b: got_ref[4, 9, b, t])
                elif s in got:
                    loads.append(lambda t, s=s, b=b: got_ref[s - 1, e, b, t])
                else:
                    loads.append(None)
        masks = [(lane >= az) & (lane < az + 32) for _, az in pairs]
        for half in range(2):
            columns = []
            for t in (2 * half, 2 * half + 1):
                rows = []
                for k, load in enumerate(loads):
                    if load is None:
                        rows += [blank] * 4
                        continue
                    value = load(t)
                    for j in range(4):
                        moved = pltpu.roll(value, lax.rem(pairs[k][1] + 128 - 32 * j, 128), 1)
                        rows.append(jnp.where(masks[k], moved, 0.0))
                columns.append(jnp.concatenate(rows, axis=0))
            placed = dot_left(sel_ref[which], jnp.concatenate(columns, axis=1))
            out_ref[e, 2 * half] = placed[:, :128]
            out_ref[e, 2 * half + 1] = placed[:, 128:]

    plane(0, 0, False, (1, 2, 3, 4), False)

    def step(e, carry):
        plane(e, 0, True, (1, 2, 3, 4), False)
        return carry

    lax.fori_loop(1, 8, step, 0)
    plane(8, 0, True, (1, 2, 3), False)
    plane(9, 1, True, (1, 2, 3), True)


def cycle_kernel(
    f_ref, r0_ref, r1_ref, p1_ref, p0_ref, fz_ref, bz_ref, fy_ref, by_ref, kx_ref, inv_ref,
    pot_ref, margin_ref,
    rim, low, fp, f1p, f2p, v0, v1p, w1, v2p, w2, tmp, tmp1, qs, qr, gs, gall, us, ur,
    send, recv, gsend, grecv,
):
    gx, gy = lax.axis_index("gx"), lax.axis_index("gy")
    n, m = lax.axis_size("gx"), lax.axis_size("gy")
    east, west = lax.rem(gx + 1, n), lax.rem(gx + n - 1, n)
    north, south = lax.rem(gy + 1, m), lax.rem(gy + m - 1, m)

    barrier = pltpu.get_barrier_semaphore()
    for d in range(1, m):
        pl.semaphore_signal(barrier, inc=1, device_id=(gx, lax.rem(gy + d, m)), device_id_type=MESH)
    for x in (east, west):
        for y in (north, south):
            pl.semaphore_signal(barrier, inc=1, device_id=(x, y), device_id_type=MESH)

    def greet(d, carry):
        pl.semaphore_signal(barrier, inc=1, device_id=(lax.rem(gx + d, n), gy), device_id_type=MESH)
        return carry

    lax.fori_loop(1, n, greet, 0)
    pl.semaphore_wait(barrier, m - 1 + 4 + n - 1)

    def copy(src, dst, slot, x, y):
        return pltpu.make_async_remote_copy(
            src_ref=src, dst_ref=dst, send_sem=send.at[slot], recv_sem=recv.at[slot],
            device_id=(x, y), device_id_type=MESH,
        )

    copies = [
        copy(f_ref.at[:, :, pl.ds(120, 40), :], rim, 0, gx, north),
        copy(f_ref.at[:, :, pl.ds(0, 8), :], low, 1, gx, south),
    ]
    for c in copies:
        c.start()
    for c in copies:
        c.wait()

    def join(e, carry):
        for t in range(4):
            fp[e, t, 0:8] = rim[e, t, 0:8]
            fp[e, t, 8:40] = f_ref[e, t, 0:32] + rim[e, t, 8:40]
            fp[e, t, 40:136] = f_ref[e, t, 32:128]
            fp[e, t, 136:144] = f_ref[e, t, 128:136] + low[e, t]
        return carry

    lax.fori_loop(0, 10, join, 0)

    scale = DAMPING / center_of(0)

    def down0(xc, carry):
        for p in range(2):
            halves = []
            for t in (2 * p, 2 * p + 1):
                total = None
                for x in range(2):
                    e = 2 * xc + 1 + x
                    mid = fp[e, t, 8:136]
                    beside = fp[e, t, 7:135] + fp[e, t, 9:137] + fp[e - 1, t, 8:136] + fp[e + 1, t, 8:136]
                    beside = beside + z_beside(mid, 128)
                    res = (1.0 - DAMPING) * mid + scale * beside
                    total = res if total is None else total + res
                tmp[0:128, :] = total
                halves.append(tmp[pl.ds(0, 64, stride=2), :] + tmp[pl.ds(1, 64, stride=2), :])
            f1p[2 + xc, p, 8:72] = dot_right(jnp.concatenate(halves, axis=1), r0_ref[...])
        return carry

    lax.fori_loop(0, 4, down0, 0)

    def swap(buf, a, c, slot):
        lead = (slice(None),) * (len(buf.shape) - 3)

        def part(x0, nx, y0, ny):
            return buf.at[(pl.ds(x0, nx),) + lead + (pl.ds(y0, ny),)]

        hi_x, lo_x, hi_y, lo_y = a, 2, c, 8
        return [
            copy(part(hi_x, 2, 8, c), part(0, 2, 8, c), slot, east, gy),
            copy(part(lo_x, 2, 8, c), part(a + 2, 2, 8, c), slot + 1, west, gy),
            copy(part(2, a, hi_y, 8), part(2, a, 0, 8), slot + 2, gx, north),
            copy(part(2, a, lo_y, 8), part(2, a, c + 8, 8), slot + 3, gx, south),
            copy(part(hi_x, 2, hi_y, 8), part(0, 2, 0, 8), slot + 4, east, north),
            copy(part(hi_x, 2, lo_y, 8), part(0, 2, c + 8, 8), slot + 5, east, south),
            copy(part(lo_x, 2, hi_y, 8), part(a + 2, 2, 0, 8), slot + 6, west, north),
            copy(part(lo_x, 2, lo_y, 8), part(a + 2, 2, c + 8, 8), slot + 7, west, south),
        ]

    copies = swap(f1p, 4, 64, 2)
    for c in copies:
        c.start()
    for c in copies:
        c.wait()

    scale = DAMPING / center_of(1) / 4.0
    for xc in range(2):
        total = None
        for p in range(2):
            both = None
            for x in range(2):
                e = 2 + 2 * xc + x
                mid = f1p[e, p, 8:72]
                beside = f1p[e, p, 7:71] + f1p[e, p, 9:73] + f1p[e - 1, p, 8:72] + f1p[e + 1, p, 8:72]
                beside = beside + z_beside(mid, 64)
                res = (1.0 - DAMPING) * mid + scale * beside
                both = res if both is None else both + res
            tmp[0:64, :] = both
            pair = tmp[pl.ds(0, 32, stride=2), :] + tmp[pl.ds(1, 32, stride=2), :]
            part = dot_right(pair, r1_ref[p])
            total = part if total is None else total + part
        f2p[2 + xc, 8:40] = total

    copies = swap(f2p, 2, 32, 10)
    for c in copies:
        c.start()
    for c in copies:
        c.wait()

    scale = DAMPING / center_of(2) / 16.0
    total = None
    for x in range(2):
        e = 2 + x
        mid = f2p[e, 8:40]
        beside = f2p[e, 7:39] + f2p[e, 9:41] + f2p[e - 1, 8:40] + f2p[e + 1, 8:40]
        beside = beside + z_beside(mid, 32)
        res = (1.0 - DAMPING) * mid + scale * beside
        total = res if total is None else total + res
    modes = dot_high(total, fz_ref[...])
    modes = jnp.concatenate([modes, jnp.zeros((96, 128), F32)], axis=0)
    modes = dot_high(fy_ref[gy], modes)
    for q in range(m):
        qs[q] = modes[16 * q : 16 * q + 8] + pltpu.roll(modes[16 * q + 8 : 16 * q + 16], 64, 1)
    copies = []
    for d in range(1, m):
        to = lax.rem(gy + d, m)
        copies.append(copy(qs.at[to], qr.at[d - 1], 17 + d, gx, to))
    for c in copies:
        c.start()
    mine = qs[gy]
    for c in copies:
        c.wait()
    for d in range(1, m):
        mine = mine + qr[d - 1]
    gs[...] = mine

    def shout(d):
        return pltpu.make_async_remote_copy(
            src_ref=gs, dst_ref=gall.at[gx], send_sem=gsend.at[d], recv_sem=grecv.at[d],
            device_id=(lax.rem(gx + d, n), gy), device_id_type=MESH,
        )

    def begin(d, carry):
        shout(d).start()
        return carry

    def end(d, carry):
        shout(d).wait()
        return carry

    lax.fori_loop(1, n, begin, 0)
    gall[gx] = mine
    lax.fori_loop(1, n, end, 0)
    spectrum = dot_high(kx_ref[...], gall[...].reshape(8 * n, 128)) * inv_ref[gy]
    for s, x in enumerate((west, gx, east)):
        us[s] = dot_high(kx_ref[pl.ds(pl.multiple_of(8 * x, 8), 8), :], spectrum)

    copies = []
    for d in range(1, m):
        to = lax.rem(gy + d, m)
        copies.append(copy(us, ur.at[gy], 21 + d, gx, to))
    for c in copies:
        c.start()
    ur[gy] = us[...]
    for c in copies:
        c.wait()

    scale = DAMPING / center_of(2)
    for s in range(3):
        rows = []
        for q in range(m):
            half = ur[q, s]
            rows += [half, pltpu.roll(half, 64, 1)]
        if m < 8:
            rows.append(jnp.zeros((128 - 16 * m, 128), F32))
        ahead = dot_high(by_ref[gy], jnp.concatenate(rows, axis=0))
        ahead = dot_high(ahead, bz_ref[...])
        for x in range(2):
            v2p[2 * s + x] = scale * f2p[2 * s + x] + ahead
    for e in range(1, 5):
        mid = v2p[e]
        beside = v2p[e - 1] + v2p[e + 1] + pltpu.roll(mid, 1, 0) + pltpu.roll(mid, 47, 0)
        beside = beside + z_beside(mid, 32)
        w2[e - 1] = (1.0 - DAMPING) * mid + scale * f2p[e] + (scale / 16.0) * beside

    scale = DAMPING / center_of(1)
    for e in range(4):
        for p in range(2):
            wide = dot_right(w2[e, 4:44], p1_ref[p])
            tmp[pl.ds(0, 40, stride=2), :] = wide
            tmp[pl.ds(1, 40, stride=2), :] = wide
            for x in range(2):
                v1p[2 * e + x, p] = scale * f1p[2 * e + x, p] + tmp[0:80, :]

    def up1(e, carry):
        for p in range(2):
            mid = v1p[e, p]
            beside = v1p[e - 1, p] + v1p[e + 1, p] + pltpu.roll(mid, 1, 0) + pltpu.roll(mid, 79, 0)
            beside = beside + z_beside(mid, 64)
            w1[e - 1, p] = (1.0 - DAMPING) * mid + scale * f1p[e, p] + (scale / 4.0) * beside
        return carry

    lax.fori_loop(1, 7, up1, 0)

    scale = DAMPING / center_of(0)

    def widen(i, p):
        wide = dot_right(w1[i, p, 4:76], p0_ref[...])
        tmp1[0, pl.ds(0, 72, stride=2), :] = wide[:, :128]
        tmp1[0, pl.ds(1, 72, stride=2), :] = wide[:, :128]
        tmp1[1, pl.ds(0, 72, stride=2), :] = wide[:, 128:]
        tmp1[1, pl.ds(1, 72, stride=2), :] = wide[:, 128:]

    for i, e in ((0, 0), (5, 9)):
        for p in range(2):
            widen(i, p)
            for t in range(2):
                v0[e, 2 * p + t] = scale * fp[e, 2 * p + t] + tmp1[t]

    def raise0(i, carry):
        for p in range(2):
            widen(i, p)
            for x in range(2):
                for t in range(2):
                    v0[2 * i - 1 + x, 2 * p + t] = scale * fp[2 * i - 1 + x, 2 * p + t] + tmp1[t]
        return carry

    lax.fori_loop(1, 5, raise0, 0)

    def up0(e, carry):
        for t in range(4):
            mid = v0[e, t, 8:136]
            beside = v0[e, t, 7:135] + v0[e, t, 9:137] + v0[e - 1, t, 8:136] + v0[e + 1, t, 8:136]
            beside = beside + z_beside(mid, 128)
            pot_ref[t, e - 1] = (1.0 - DAMPING) * mid + scale * (fp[e, t, 8:136] + beside)
        return carry

    lax.fori_loop(1, 9, up0, 0)
    last = copy(pot_ref.at[:, :, pl.ds(0, 32), :], margin_ref, 26, gx, south)
    last.start()
    last.wait()


def window_kernel(anc_ref, ganc_ref, pot_ref, margin_ref, out_ref, win_ref, sel_ref):
    pairs = box_anchors(anc_ref, ganc_ref, [-1, 0, 1, 2, 3])
    row = lax.broadcasted_iota(jnp.int32, (320, 160), 0)
    col = lax.broadcasted_iota(jnp.int32, (320, 160), 1)
    want = 4 * (row % 8) + (row // 8) % 4
    box = row // 32
    for k, (ay, _) in enumerate(pairs):
        want = want + jnp.where(box == k, ay, 0)
    sel_ref[...] = jnp.where(col == want, 1.0, 0.0).astype(BF16)
    group = lax.broadcasted_iota(jnp.int32, (8, 128), 1) // 32

    def plane(x, carry):
        for half in range(2):
            columns = []
            for t in (2 * half, 2 * half + 1):
                here = pot_ref[t, x]
                out_ref[t, x] = here
                columns.append(jnp.concatenate([here, margin_ref[t, x]], axis=0))
            taken = dot_left(sel_ref[...], jnp.concatenate(columns, axis=1))
            for u in range(2):
                for k in range(10):
                    total = None
                    for j in range(4):
                        piece = taken[32 * k + 8 * j : 32 * k + 8 * j + 8, 128 * u : 128 * u + 128]
                        piece = pltpu.roll(piece, lax.rem(128 + 32 * j - pairs[k][1], 128), 1)
                        total = piece if total is None else jnp.where(group == j, piece, total)
                    win_ref[k // 2, x, k % 2, 2 * half + u] = total
        return carry

    lax.fori_loop(0, 8, plane, 0)


def return_kernel(src_ref, got_ref, send, recv):
    gx, gy = lax.axis_index("gx"), lax.axis_index("gy")
    n = lax.axis_size("gx")
    barrier = pltpu.get_barrier_semaphore()
    for k in range(1, 5):
        pl.semaphore_signal(barrier, inc=1, device_id=(lax.rem(gx + k, n), gy), device_id_type=MESH)
    pl.semaphore_wait(barrier, 4)
    copies = []
    for k in range(1, 5):
        copies.append(
            pltpu.make_async_remote_copy(
                src_ref=src_ref.at[k],
                dst_ref=got_ref.at[k - 1],
                send_sem=send.at[k - 1],
                recv_sem=recv.at[k - 1],
                device_id=(lax.rem(gx - k + n, n), gy),
                device_id_type=MESH,
            )
        )
    for c in copies:
        c.start()
    for c in copies:
        c.wait()


def project_kernel(ax_ref, occ_ref, vir_ref, own_ref, got_ref, out_ref, win):
    win[0:8] = own_ref[0]
    for k in range(4):
        win[8 * k + 8 : 8 * k + 16] = got_ref[k]
    for b in range(2):

        def step(s, total, b=b):
            left, right = [], []
            for h in range(4):
                rows = pl.ds(pl.multiple_of(s * 64 + 16 * h, 16), 16)
                occ = occ_ref[b, :, rows, :].astype(F32)
                vir = vir_ref[b, :, rows, :].astype(F32)
                for g in range(2):
                    cells = win[ax_ref[b] + s * 8 + 2 * h + g, b]
                    weighted = occ[None, :, 8 * g : 8 * g + 8] * cells[:, None]
                    left.append(weighted.reshape(256, 128).astype(BF16))
                    right.append(vir[:, 8 * g : 8 * g + 8].reshape(64, 128).astype(BF16))
            left, right = jnp.concatenate(left, axis=1), jnp.concatenate(right, axis=1)
            return total + lax.dot_general(
                left, right, (((1,), (1,)), ((), ())), preferred_element_type=F32
            )

        total = lax.fori_loop(0, 4, step, jnp.zeros((256, 64), F32))
        row = lax.broadcasted_iota(jnp.int32, (256, 64), 0) % 8
        col = lax.broadcasted_iota(jnp.int32, (256, 64), 1) % 8
        total = jnp.where(row == col, total, 0.0)
        total = jnp.sum(total.reshape(32, 8, 64), axis=1)
        col = lax.broadcasted_iota(jnp.int32, (64, 128), 1)
        row = lax.broadcasted_iota(jnp.int32, (64, 128), 0) // 8
        pick = jnp.where(row == col, float(BOX) ** (-1.5), 0.0)
        out_ref[b] = dot_high(total, pick)


def params(**more):
    return pltpu.CompilerParams(vmem_limit_bytes=40 * 1024 * 1024, **more)


def shaped(shape, dtype=F32):
    return jax.ShapeDtypeStruct(shape, dtype)


def per_device(slabs, tiles, occupied, virtual, trials, anchor_x, anchor_y, anchor_z):
    occ = occupied.reshape(2, 8, 256, 128)
    vir = virtual.reshape(2, 8, 256, 128)
    mix = jnp.einsum("btia,mn->bitman", trials, jnp.eye(8, dtype=BF16)).reshape(2, 256, 64)
    anchors = jnp.concatenate([anchor_y, anchor_z, jnp.zeros((124,), jnp.int32)])
    anchors = jnp.broadcast_to(anchors[None], (8, 128))
    tab = tables(slabs, tiles)
    exact = {k: jnp.asarray(tab[k], BF16) for k in ("r0", "r1", "p1", "p0")}
    wide = {k: jnp.asarray(tab[k], F32) for k in ("fz", "bz", "fy", "by", "kx", "inv")}

    dens = pl.pallas_call(
        density_kernel,
        out_shape=shaped((40, 2, 4, 8, 128)),
        in_specs=[SMEM, VMEM, VMEM, VMEM],
        out_specs=VMEM,
        compiler_params=params(),
        name="density",
    )(anchor_x, occ, vir, mix)

    got, ganc = pl.pallas_call(
        deposit_kernel,
        out_shape=(shaped((5, 10, 2, 4, 8, 128)), shaped((5, 8, 128), jnp.int32)),
        in_specs=[ANY, ANY],
        out_specs=(ANY, ANY),
        scratch_shapes=[pltpu.SemaphoreType.DMA((10,)), pltpu.SemaphoreType.DMA((10,))],
        compiler_params=params(collective_id=0, has_side_effects=True),
        name="deposit",
    )(dens, anchors)

    grid = pl.pallas_call(
        accumulate_kernel,
        out_shape=shaped((10, 4, 160, 128)),
        in_specs=[SMEM, SMEM, VMEM, VMEM],
        out_specs=VMEM,
        scratch_shapes=[pltpu.VMEM((2, 160, 320), BF16)],
        compiler_params=params(),
        name="accumulate",
    )(anchors, ganc, dens, got)

    names = ("r0", "r1", "p1", "p0")
    others = ("fz", "bz", "fy", "by", "kx", "inv")
    pot, margin = pl.pallas_call(
        cycle_kernel,
        out_shape=(shaped((4, 8, 128, 128)), shaped((4, 8, 32, 128))),
        in_specs=[VMEM] * 11,
        out_specs=(VMEM, VMEM),
        scratch_shapes=[
            pltpu.VMEM((10, 4, 40, 128), F32),
            pltpu.VMEM((10, 4, 8, 128), F32),
            pltpu.VMEM((10, 4, 144, 128), F32),
            pltpu.VMEM((8, 2, 80, 128), F32),
            pltpu.VMEM((6, 48, 128), F32),
            pltpu.VMEM((10, 4, 144, 128), F32),
            pltpu.VMEM((8, 2, 80, 128), F32),
            pltpu.VMEM((6, 2, 80, 128), F32),
            pltpu.VMEM((6, 48, 128), F32),
            pltpu.VMEM((4, 48, 128), F32),
            pltpu.VMEM((144, 128), F32),
            pltpu.VMEM((2, 144, 128), F32),
            pltpu.VMEM((tiles, 8, 128), F32),
            pltpu.VMEM((tiles, 8, 128), F32),
            pltpu.VMEM((8, 128), F32),
            pltpu.VMEM((slabs, 8, 128), F32),
            pltpu.VMEM((3, 8, 128), F32),
            pltpu.VMEM((tiles, 3, 8, 128), F32),
            pltpu.SemaphoreType.DMA((28,)),
            pltpu.SemaphoreType.DMA((28,)),
            pltpu.SemaphoreType.DMA((slabs,)),
            pltpu.SemaphoreType.DMA((slabs,)),
        ],
        compiler_params=params(collective_id=1, has_side_effects=True),
        name="cycle",
    )(grid, *[exact[k] for k in names], *[wide[k] for k in others])

    potential, windows = pl.pallas_call(
        window_kernel,
        out_shape=(shaped((4, 8, 128, 128)), shaped((5, 8, 2, 4, 8, 128))),
        in_specs=[SMEM, SMEM, VMEM, VMEM],
        out_specs=(VMEM, VMEM),
        scratch_shapes=[pltpu.VMEM((320, 160), BF16)],
        compiler_params=params(),
        name="window",
    )(anchors, ganc, pot, margin)

    back = pl.pallas_call(
        return_kernel,
        out_shape=shaped((4, 8, 2, 4, 8, 128)),
        in_specs=[ANY],
        out_specs=ANY,
        scratch_shapes=[pltpu.SemaphoreType.DMA((4,)), pltpu.SemaphoreType.DMA((4,))],
        compiler_params=params(collective_id=2, has_side_effects=True),
        name="send_back",
    )(windows)

    coupling = pl.pallas_call(
        project_kernel,
        out_shape=shaped((2, 32, 128)),
        in_specs=[SMEM, VMEM, VMEM, VMEM, VMEM],
        out_specs=VMEM,
        scratch_shapes=[pltpu.VMEM((40, 2, 4, 8, 128), F32)],
        compiler_params=params(),
        name="project",
    )(anchor_x, occ, vir, windows, back)
    return potential, coupling[:, :, :8].reshape(2, 4, 8, 8)


def solution(mesh):
    placed = (
        P(("gx", "gy"), None, None),
        P(("gx", "gy"), None, None),
        P(("gx", "gy"), None, None, None),
        P(("gx", "gy")),
        P(("gx", "gy")),
        P(("gx", "gy")),
    )
    return jax.shard_map(
        functools.partial(per_device, mesh.shape["gx"], mesh.shape["gy"]),
        mesh=mesh,
        in_specs=placed,
        out_specs=(P(None, "gx", "gy", None), P(("gx", "gy"), None, None, None)),
        check_vma=False,
    )
```

time: 1070 us -> 148 us (0.14); the launches traced: 1060 us -> 148 us
  waiting for transfers between devices: 319 us -> 0 us
  starting transfers between devices: 244 us -> 0 us
  local copies, waits for them, and re-layouts: 202 us -> 3.84 us
  blocking collectives: 171 us -> 0 us
  Pallas kernels: 0 us -> 142 us
  other arithmetic: 85.1 us -> 1.35 us
  matrix products: 22.9 us -> 0 us
  between operations: 12.8 us -> 0.9 us
    ppermute x34 -> x0, waiting for transfers between devices: 319 us -> none  [the longest x10 281 us: passed_along(): lax.ppermute(x, axis, [(i, (i + by) % length) for i in range(length)])]
    ppermute x34 -> x0, starting transfers between devices: 244 us -> none  [the longest x10 107 us: passed_along(): lax.ppermute(x, axis, [(i, (i + by) % length) for i in range(length)])]
    all_gather x1 -> x0, blocking collectives: 171 us -> none  [coarse_solve(): everything = lax.all_gather(flat, ('gx', 'gy'), axis=0, tiled=True)]
    pallas_call x0 -> x7, Pallas kernels: none -> 142 us  [the longest x1 71 us: per_device(): pl.pallas_call(cycle_kernel, out_shape=(shaped((4, 8, 128, 128)), shaped(...]
    dynamic_update_slice x2 -> x0, local copies, waits for them, and re-layouts: 99.3 us -> none  [per_device(): extended = lax.dynamic_update_slice(extended, block, spot)]
    reduce_sum x4 -> x0, other arithmetic: 57.1 us -> none  [restrict(): return blocks.mean(axis=(2, 4, 6))]
    sub x2 -> x0, local copies, waits for them, and re-layouts: 38.8 us -> none  [vcycle(): residue = source - operate(first, spacing)]
    dot_general x10 -> x0, matrix products: 22.9 us -> none  [the longest x2 8.56 us: transform_all(): return jnp.einsum('tabz,zc->tabc', field, table_z, precision=high)]
  transfers between devices with their start and end apart: 34 -> 0, of which waited for: 26 -> 0; matrix products, arithmetic and copies ran while one was open for 1% -> 0% of each run, Pallas kernels for 0% -> 0%
where the time goes in v1:
time: 148 us
  Pallas kernels  142 us (96%)
  local copies, waits for them, and re-layouts  3.84 us (3%)
    pallas_call x1, Pallas kernels, per_device(): pl.pallas_call(cycle_kernel, out_shape=(shaped((4, 8, 128, 128)), shaped(...  71 us
    pallas_call x1, Pallas kernels, per_device(): pl.pallas_call(return_kernel, out_shape=shaped((4, 8, 2, 4, 8, 128)), in_...  26.8 us
    pallas_call x1, Pallas kernels, per_device(): pl.pallas_call(deposit_kernel, out_shape=(shaped((5, 10, 2, 4, 8, 128)),...  22.7 us
    pallas_call x1, Pallas kernels, per_device(): pl.pallas_call(density_kernel, out_shape=shaped((40, 2, 4, 8, 128)), in_s...  6.22 us
    pallas_call x1, Pallas kernels, per_device(): pl.pallas_call(window_kernel, out_shape=(shaped((4, 8, 128, 128)), shaped...  6.2 us
    pallas_call x1, Pallas kernels, per_device(): pl.pallas_call(accumulate_kernel, out_shape=shaped((10, 4, 160, 128)), in...  5.71 us
    pallas_call x1, Pallas kernels, per_device(): pl.pallas_call(project_kernel, out_shape=shaped((2, 32, 128)), in_specs=[...  3.45 us

profile of v1, /device:TPU:7, one launch (start us, length us, event | category | flops | bytes accessed | tf_op | source)
XLA Modules:
  0.0 148.1 jit_solution(11038031506562173958)
XLA Ops:
  0.7 0.9 pad_add_fusion
  1.6 0.9 copy.19
  2.5 0.5 multiply_bitcast_fusion
  2.9 1.5 reshape.19
  4.4 0.1 copy.20.mix_ref
  4.5 0.5 copy_bitcast_fusion
  5.0 0.2 copy-done.10
  5.2 6.2 %density.1.src_ref.own_ref = f32[40,2,4,8,128]{4,3,2,1,0:T(8,128)S(1)} custom-call(s32[2]{0:T(128)S(1)} %copy-done.10, bf16[2,8,256,128]{3,2,1,0:T(8,128)(2,1)S(1)} %get-tuple-element.15.occ_ref, bf16[2,8,256,128]{3,2,1,0:T(8,128)(2,1)S(1)} %get-tuple-element.14.vir_ref, bf16[2,256,64]{2,1,0:T(8,128)(2,1)S(1)} %copy.20.mix_ref), custom_call_target="tpu_custom_call" | custom-call | tf_op jit(solution)/shard_map/density/pallas_call | solution.py:623
  11.4 22.7 %deposit.1 = (f32[5,10,2,4,8,128]{5,4,3,2,1,0:T(8,128)S(1)}, s32[5,8,128]{2,1,0:T(8,128)S(1)}) custom-call(f32[40,2,4,8,128]{4,3,2,1,0:T(8,128)S(1)} %density.1.src_ref.own_ref, s32[8,128]{1,0:T(8,128)S(1)} %broadcast_in_dim.10.anc_ref), custom_call_target="tpu_custom_call" | custom-call | tf_op jit(solution)/shard_map/deposit/pallas_call | solution.py:632
  34.1 0.0 copy-start
  34.1 0.0 copy-start.1
  34.1 0.0 copy-start.2
  34.1 0.0 copy-start.3
  34.1 0.0 copy-start.4
  34.2 0.0 copy-start.5
  34.2 0.0 copy-start.7
  34.2 0.0 copy-start.8
  34.2 0.0 copy-start.9
  34.2 5.7 %accumulate.1.f_ref = f32[10,4,160,128]{3,2,1,0:T(8,128)S(1)} custom-call(s32[8,128]{1,0:T(8,128)S(1)} %broadcast_in_dim.10.anc_ref, s32[5,8,128]{2,1,0:T(8,128)S(1)} %get-tuple-element.8.ganc_ref, f32[40,2,4,8,128]{4,3,2,1,0:T(8,128)S(1)} %density.1.src_ref.own_ref, f32[5,10,2,4,8,128]{5,4,3,2,1,0:T(8,128)S(1)} %get-tuple-element.9.got_ref), custom_call_target="tpu_custom_call" | custom-call | tf_op jit(solution)/shard_map/accumulate/pallas_call | solution.py:642
  40.0 71.0 %cycle.1 = (f32[4,8,128,128]{3,2,1,0:T(8,128)S(1)}, f32[4,8,32,128]{3,2,1,0:T(8,128)S(1)}) custom-call(f32[10,4,160,128]{3,2,1,0:T(8,128)S(1)} %accumulate.1.f_ref, bf16[256,128]{1,0:T(8,128)(2,1)S(1)} %copy-done.9, bf16[2,128,128]{2,1,0:T(8,128)(2,1)S(1)} %copy-done.8, bf16[2,128,128]{2,1,0:T(8,128)(2,1)S(1)} %copy-done.7, bf16[128,256]{1,0:T(8,128)(2,1)S(1)} %copy-done.6, ...), custom_call_target="tpu_custom_call" | custom-call | tf_op jit(solution)/shard_map/cycle/pallas_call | solution.py:654
  111.0 6.2 %window.1 = (f32[4,8,128,128]{3,2,1,0:T(8,128)}, f32[5,8,2,4,8,128]{5,4,3,2,1,0:T(8,128)S(1)}) custom-call(s32[8,128]{1,0:T(8,128)S(1)} %broadcast_in_dim.10.anc_ref, s32[5,8,128]{2,1,0:T(8,128)S(1)} %get-tuple-element.8.ganc_ref, f32[4,8,128,128]{3,2,1,0:T(8,128)S(1)} %get-tuple-element.10.pot_ref, f32[4,8,32,128]{3,2,1,0:T(8,128)S(1)} %get-tuple-element.11.margin_ref), custom_call_target="tpu_custom_call" | custom-call | tf_op jit(solution)/shard_map/window/pallas_call | solution.py:687
  117.2 26.8 %send_back.1.got_ref = f32[4,8,2,4,8,128]{5,4,3,2,1,0:T(8,128)S(1)} custom-call(f32[5,8,2,4,8,128]{5,4,3,2,1,0:T(8,128)S(1)} %get-tuple-element.13.src_ref.own_ref), custom_call_target="tpu_custom_call" | custom-call | tf_op jit(solution)/shard_map/send_back/pallas_call | solution.py:697
  144.0 3.4 %project.1 = f32[2,32,128]{2,1,0:T(8,128)S(1)} custom-call(s32[2]{0:T(128)S(1)} %copy-done.10, bf16[2,8,256,128]{3,2,1,0:T(8,128)(2,1)S(1)} %get-tuple-element.15.occ_ref, bf16[2,8,256,128]{3,2,1,0:T(8,128)(2,1)S(1)} %get-tuple-element.14.vir_ref, f32[5,8,2,4,8,128]{5,4,3,2,1,0:T(8,128)S(1)} %get-tuple-element.13.src_ref.own_ref, ...), custom_call_target="tpu_custom_call" | custom-call | tf_op jit(solution)/shard_map/project/pallas_call | solution.py:707
  147.5 0.6 slice_bitcast_fusion
  (19 shorter events, 0.0 us)
Async XLA Ops:
  0.6 3.9 %copy-start.11 = (bf16[2,8,32768]{2,1,0:T(8,128)(2,1)S(1)}, bf16[2,8,32768]{2,1,0:T(8,128)(2,1)}, u32[]{:S(2)}) copy-start(bf16[2,8,32768]{2,1,0:T(8,128)(2,1)} %param.17) | copy-start | bytes 3145732
  0.6 3.9 %copy-start.12 = (bf16[2,8,32768]{2,1,0:T(8,128)(2,1)S(1)}, bf16[2,8,32768]{2,1,0:T(8,128)(2,1)}, u32[]{:S(2)}) copy-start(bf16[2,8,32768]{2,1,0:T(8,128)(2,1)} %param.16) | copy-start | bytes 3145732
  4.5 0.7 copy-start.10
  34.1 5.8 %copy-start = (f32[4,256,128]{2,1,0:T(8,128)S(1)}, f32[4,256,128]{2,1,0:T(8,128)}, u32[]{:S(2)}) copy-start(f32[4,256,128]{2,1,0:T(8,128)} %constant.31.clone.inv_ref) | copy-start | bytes 1572868
  34.1 5.8 %copy-start.1 = (f32[256,256]{1,0:T(8,128)S(1)}, f32[256,256]{1,0:T(8,128)}, u32[]{:S(2)}) copy-start(f32[256,256]{1,0:T(8,128)} %constant.30.clone.kx_ref) | copy-start | bytes 786436
  34.1 5.8 %copy-start.2 = (f32[4,64,128]{2,1,0:T(8,128)S(1)}, f32[4,64,128]{2,1,0:T(8,128)}, u32[]{:S(2)}) copy-start(f32[4,64,128]{2,1,0:T(8,128)} %constant.28.clone.fy_ref) | copy-start | bytes 393220
  34.1 5.8 %copy-start.3 = (f32[4,48,128]{2,1,0:T(8,128)S(1)}, f32[4,48,128]{2,1,0:T(8,128)}, u32[]{:S(2)}) copy-start(f32[4,48,128]{2,1,0:T(8,128)} %constant.29.clone.by_ref) | copy-start | bytes 294916
  34.1 5.8 %copy-start.4 = (f32[128,128]{1,0:T(8,128)S(1)}, f32[128,128]{1,0:T(8,128)}, u32[]{:S(2)}) copy-start(f32[128,128]{1,0:T(8,128)} %constant.27.clone.bz_ref) | copy-start | bytes 196612
  34.2 5.8 %copy-start.5 = (f32[128,128]{1,0:T(8,128)S(1)}, f32[128,128]{1,0:T(8,128)}, u32[]{:S(2)}) copy-start(f32[128,128]{1,0:T(8,128)} %constant.26.clone.fz_ref) | copy-start | bytes 196612
  34.2 5.8 %copy-start.6 = (bf16[128,256]{1,0:T(8,128)(2,1)S(1)}, bf16[128,256]{1,0:T(8,128)(2,1)}, u32[]{:S(2)}) copy-start(bf16[128,256]{1,0:T(8,128)(2,1)} %constant.25.clone.p0_ref) | copy-start | bytes 196612
  34.2 5.8 %copy-start.7 = (bf16[2,128,128]{2,1,0:T(8,128)(2,1)S(1)}, bf16[2,128,128]{2,1,0:T(8,128)(2,1)}, u32[]{:S(2)}) copy-start(bf16[2,128,128]{2,1,0:T(8,128)(2,1)} %constant.24.clone.p1_ref) | copy-start | bytes 196612
  34.2 5.8 %copy-start.8 = (bf16[2,128,128]{2,1,0:T(8,128)(2,1)S(1)}, bf16[2,128,128]{2,1,0:T(8,128)(2,1)}, u32[]{:S(2)}) copy-start(bf16[2,128,128]{2,1,0:T(8,128)(2,1)} %constant.23.clone.r1_ref) | copy-start | bytes 196612
  34.2 5.8 %copy-start.9 = (bf16[256,128]{1,0:T(8,128)(2,1)S(1)}, bf16[256,128]{1,0:T(8,128)(2,1)}, u32[]{:S(2)}) copy-start(bf16[256,128]{1,0:T(8,128)(2,1)} %constant.22.clone.r0_ref) | copy-start | bytes 196612

commit v2 on v1

--- a/solution.py
+++ b/solution.py
@@ -149,43 +149,73 @@
         lax.fori_loop(0, 16, step, 0)
 
 
-def deposit_kernel(src_ref, anc_ref, got_ref, ganc_ref, send, recv):
+def greet_slabs(gx, gy, n):
+    barrier = pltpu.get_barrier_semaphore()
+    for k in (-4, -3, -2, -1, 1, 2, 3, 4):
+        pl.semaphore_signal(barrier, inc=1, device_id=(lax.rem(gx + k + n, n), gy), device_id_type=MESH)
+    pl.semaphore_wait(barrier, 8)
+
+
+def shift_slabs(sign, pieces, relays, send, recv):
     gx, gy = lax.axis_index("gx"), lax.axis_index("gy")
     n = lax.axis_size("gx")
-    targets = [1, 2, 3, 4, -1]
-    barrier = pltpu.get_barrier_semaphore()
-    for k in targets:
-        pl.semaphore_signal(barrier, inc=1, device_id=(lax.rem(gx - k + n, n), gy), device_id_type=MESH)
-    pl.semaphore_wait(barrier, 5)
-    pieces = [(7, 10, 0), (15, 10, 0), (23, 10, 0), (31, 8, 0), (0, 1, 9)]
-    copies = []
-    for s, k in enumerate(targets):
-        first, count, to = pieces[s]
-        where = (lax.rem(gx + k + n, n), gy)
-        copies.append(
-            pltpu.make_async_remote_copy(
-                src_ref=anc_ref,
-                dst_ref=ganc_ref.at[s],
-                send_sem=send.at[5 + s],
-                recv_sem=recv.at[5 + s],
-                device_id=where,
-                device_id_type=MESH,
-            )
+    place = lax.rem(gx, 4) if sign > 0 else 3 - lax.rem(gx, 4)
+
+    def copy(src, dst, slot, k):
+        return pltpu.make_async_remote_copy(
+            src_ref=src, dst_ref=dst, send_sem=send.at[slot], recv_sem=recv.at[slot],
+            device_id=(lax.rem(gx + sign * k + n, n), gy), device_id_type=MESH,
         )
-        copies.append(
-            pltpu.make_async_remote_copy(
-                src_ref=src_ref.at[pl.ds(first, count)],
-                dst_ref=got_ref.at[s, pl.ds(to, count)],
-                send_sem=send.at[s],
-                recv_sem=recv.at[s],
-                device_id=where,
-                device_id_type=MESH,
-            )
-        )
-    for c in copies:
+
+    count = len(pieces) + len(relays)
+    outs = []
+    for r, (k, src, dst, hold, least) in enumerate(relays):
+        straight = copy(src, dst, len(pieces) + r, k)
+        first = copy(src, hold, count + r, 4)
+        second = copy(hold, dst, len(pieces) + r, k - 4)
+        outs.append((straight, first, second, place >= least))
+    for straight, first, second, bent in outs:
+        pl.when(bent)(first.start)
+    whole = [copy(src, dst, p, k) for p, (k, src, dst) in enumerate(pieces)]
+    for c in whole:
         c.start()
-    for c in copies:
+    for straight, first, second, bent in outs:
+        pl.when(jnp.logical_not(bent))(straight.start)
+    for straight, first, second, bent in outs:
+
+        def onward(first=first, second=second):
+            first.wait_recv()
+            second.start()
+
+        pl.when(bent)(onward)
+    for straight, first, second, bent in outs:
+
+        def settle(first=first, second=second):
+            first.wait_send()
+            second.wait_send()
+
+        pl.when(bent)(settle)
+        pl.when(jnp.logical_not(bent))(straight.wait_send)
+        straight.wait_recv()
+    for c in whole:
         c.wait()
+
+
+def deposit_kernel(src_ref, anc_ref, got_ref, ganc_ref, hold1, hold2, send, recv):
+    gx, gy = lax.axis_index("gx"), lax.axis_index("gy")
+    greet_slabs(gx, gy, lax.axis_size("gx"))
+    pieces = [(k, anc_ref, ganc_ref.at[s]) for s, k in enumerate((1, 2, 3, 4, -1))]
+    pieces += [
+        (4, src_ref.at[pl.ds(31, 8)], got_ref.at[3, pl.ds(0, 8)]),
+        (3, src_ref.at[pl.ds(23, 10)], got_ref.at[2]),
+        (2, src_ref.at[pl.ds(15, 10), 0], got_ref.at[1, :, 0]),
+        (-1, src_ref.at[pl.ds(0, 1)], got_ref.at[4, pl.ds(9, 1)]),
+    ]
+    relays = [
+        (1, src_ref.at[pl.ds(7, 10)], got_ref.at[0], hold1, 3),
+        (2, src_ref.at[pl.ds(15, 10), 1], got_ref.at[1, :, 1], hold2, 2),
+    ]
+    shift_slabs(1, pieces, relays, send, recv)
 
 
 def box_anchors(anc_ref, ganc_ref, sources):
@@ -262,7 +292,7 @@
 def cycle_kernel(
     f_ref, r0_ref, r1_ref, p1_ref, p0_ref, fz_ref, bz_ref, fy_ref, by_ref, kx_ref, inv_ref,
     pot_ref, margin_ref,
-    rim, low, fp, f1p, f2p, v0, v1p, w1, v2p, w2, tmp, tmp1, qs, qr, gs, gall, us, ur,
+    rim, sides, beyond, fp, f1p, f2p, v0, v1p, w1, v2p, w2, tmp, tmp1, qs, qr, gs, gall, us, ur,
     send, recv, gsend, grecv,
 ):
     gx, gy = lax.axis_index("gx"), lax.axis_index("gy")
@@ -290,23 +320,40 @@
             device_id=(x, y), device_id_type=MESH,
         )
 
-    copies = [
-        copy(f_ref.at[:, :, pl.ds(120, 40), :], rim, 0, gx, north),
-        copy(f_ref.at[:, :, pl.ds(0, 8), :], low, 1, gx, south),
-    ]
-    for c in copies:
+    def edge(e, carry):
+        for t in range(4):
+            sides[0, e, t : t + 1] = f_ref[e + 1, t, 127:128]
+            sides[1, e, t : t + 1] = f_ref[e + 1, t, 0:1]
+        return carry
+
+    copies = [copy(f_ref.at[:, :, pl.ds(128, 32), :], rim, 0, gx, north)]
+    copies[0].start()
+    lax.fori_loop(0, 8, edge, 0)
+    copies += [copy(sides.at[0], beyond.at[0], 1, gx, north), copy(sides.at[1], beyond.at[1], 38, gx, south)]
+    for c in copies[1:]:
         c.start()
+
+    def early(e, carry):
+        for t in range(4):
+            fp[e, t, 40:136] = f_ref[e, t, 32:128]
+        return carry
+
+    lax.fori_loop(0, 10, early, 0)
     for c in copies:
         c.wait()
 
     def join(e, carry):
         for t in range(4):
-            fp[e, t, 0:8] = rim[e, t, 0:8]
-            fp[e, t, 8:40] = f_ref[e, t, 0:32] + rim[e, t, 8:40]
-            fp[e, t, 40:136] = f_ref[e, t, 32:128]
-            fp[e, t, 136:144] = f_ref[e, t, 128:136] + low[e, t]
-        return carry
-
+            fp[e, t, 8:40] = f_ref[e, t, 0:32] + rim[e, t]
+        return carry
+
+    def rims(e, carry):
+        for t in range(4):
+            fp[e, t, 7:8] = beyond[0, e - 1, t : t + 1]
+            fp[e, t, 136:137] = f_ref[e, t, 128:129] + beyond[1, e - 1, t : t + 1]
+        return carry
+
+    lax.fori_loop(1, 9, rims, 0)
     lax.fori_loop(0, 10, join, 0)
 
     scale = DAMPING / center_of(0)
@@ -336,23 +383,27 @@
         def part(x0, nx, y0, ny):
             return buf.at[(pl.ds(x0, nx),) + lead + (pl.ds(y0, ny),)]
 
-        hi_x, lo_x, hi_y, lo_y = a, 2, c, 8
-        return [
-            copy(part(hi_x, 2, 8, c), part(0, 2, 8, c), slot, east, gy),
-            copy(part(lo_x, 2, 8, c), part(a + 2, 2, 8, c), slot + 1, west, gy),
-            copy(part(2, a, hi_y, 8), part(2, a, 0, 8), slot + 2, gx, north),
-            copy(part(2, a, lo_y, 8), part(2, a, c + 8, 8), slot + 3, gx, south),
-            copy(part(hi_x, 2, hi_y, 8), part(0, 2, 0, 8), slot + 4, east, north),
-            copy(part(hi_x, 2, lo_y, 8), part(0, 2, c + 8, 8), slot + 5, east, south),
-            copy(part(lo_x, 2, hi_y, 8), part(a + 2, 2, 0, 8), slot + 6, west, north),
-            copy(part(lo_x, 2, lo_y, 8), part(a + 2, 2, c + 8, 8), slot + 7, west, south),
+        near = [
+            copy(part(a + 1, 1, 8, c), part(1, 1, 8, c), slot, east, gy),
+            copy(part(2, 1, 8, c), part(a + 2, 1, 8, c), slot + 1, west, gy),
+            copy(part(2, a, c, 8), part(2, a, 0, 8), slot + 2, gx, north),
+            copy(part(2, a, 8, 8), part(2, a, c + 8, 8), slot + 3, gx, south),
         ]
-
-    copies = swap(f1p, 4, 64, 2)
-    for c in copies:
-        c.start()
-    for c in copies:
-        c.wait()
+        far = [
+            copy(part(a, 1, 8, c), part(0, 1, 8, c), slot + 4, east, gy),
+            copy(part(3, 1, 8, c), part(a + 3, 1, 8, c), slot + 5, west, gy),
+            copy(part(a, 2, c, 8), part(0, 2, 0, 8), slot + 6, east, north),
+            copy(part(a, 2, 8, 8), part(0, 2, c + 8, 8), slot + 7, east, south),
+            copy(part(2, 2, c, 8), part(a + 2, 2, 0, 8), slot + 8, west, north),
+            copy(part(2, 2, 8, 8), part(a + 2, 2, c + 8, 8), slot + 9, west, south),
+        ]
+        for one in near + far:
+            one.start()
+        for one in near:
+            one.wait()
+        return far
+
+    far1 = swap(f1p, 4, 64, 2)
 
     scale = DAMPING / center_of(1) / 4.0
     for xc in range(2):
@@ -372,11 +423,7 @@
             total = part if total is None else total + part
         f2p[2 + xc, 8:40] = total
 
-    copies = swap(f2p, 2, 32, 10)
-    for c in copies:
-        c.start()
-    for c in copies:
-        c.wait()
+    far2 = swap(f2p, 2, 32, 12)
 
     scale = DAMPING / center_of(2) / 16.0
     total = None
@@ -395,7 +442,7 @@
     copies = []
     for d in range(1, m):
         to = lax.rem(gy + d, m)
-        copies.append(copy(qs.at[to], qr.at[d - 1], 17 + d, gx, to))
+        copies.append(copy(qs.at[to], qr.at[d - 1], 22 + d, gx, to))
     for c in copies:
         c.start()
     mine = qs[gy]
@@ -429,13 +476,15 @@
     copies = []
     for d in range(1, m):
         to = lax.rem(gy + d, m)
-        copies.append(copy(us, ur.at[gy], 21 + d, gx, to))
+        copies.append(copy(us, ur.at[gy], 28 + d, gx, to))
     for c in copies:
         c.start()
     ur[gy] = us[...]
     for c in copies:
         c.wait()
 
+    for c in far2:
+        c.wait()
     scale = DAMPING / center_of(2)
     for s in range(3):
         rows = []
@@ -454,6 +503,8 @@
         beside = beside + z_beside(mid, 32)
         w2[e - 1] = (1.0 - DAMPING) * mid + scale * f2p[e] + (scale / 16.0) * beside
 
+    for c in far1:
+        c.wait()
     scale = DAMPING / center_of(1)
     for e in range(4):
         for p in range(2):
@@ -507,7 +558,7 @@
         return carry
 
     lax.fori_loop(1, 9, up0, 0)
-    last = copy(pot_ref.at[:, :, pl.ds(0, 32), :], margin_ref, 26, gx, south)
+    last = copy(pot_ref.at[:, :, pl.ds(0, 32), :], margin_ref, 37, gx, south)
     last.start()
     last.wait()
 
@@ -544,29 +595,19 @@
     lax.fori_loop(0, 8, plane, 0)
 
 
-def return_kernel(src_ref, got_ref, send, recv):
+def return_kernel(src_ref, got_ref, hold1, hold2, send, recv):
     gx, gy = lax.axis_index("gx"), lax.axis_index("gy")
-    n = lax.axis_size("gx")
-    barrier = pltpu.get_barrier_semaphore()
-    for k in range(1, 5):
-        pl.semaphore_signal(barrier, inc=1, device_id=(lax.rem(gx + k, n), gy), device_id_type=MESH)
-    pl.semaphore_wait(barrier, 4)
-    copies = []
-    for k in range(1, 5):
-        copies.append(
-            pltpu.make_async_remote_copy(
-                src_ref=src_ref.at[k],
-                dst_ref=got_ref.at[k - 1],
-                send_sem=send.at[k - 1],
-                recv_sem=recv.at[k - 1],
-                device_id=(lax.rem(gx - k + n, n), gy),
-                device_id_type=MESH,
-            )
-        )
-    for c in copies:
-        c.start()
-    for c in copies:
-        c.wait()
+    greet_slabs(gx, gy, lax.axis_size("gx"))
+    pieces = [
+        (4, src_ref.at[4], got_ref.at[3]),
+        (3, src_ref.at[3], got_ref.at[2]),
+        (2, src_ref.at[2, :, 0], got_ref.at[1, :, 0]),
+    ]
+    relays = [
+        (1, src_ref.at[1], got_ref.at[0], hold1, 3),
+        (2, src_ref.at[2, :, 1], got_ref.at[1, :, 1], hold2, 2),
+    ]
+    shift_slabs(-1, pieces, relays, send, recv)
 
 
 def project_kernel(ax_ref, occ_ref, vir_ref, own_ref, got_ref, out_ref, win):
@@ -634,7 +675,12 @@
         out_shape=(shaped((5, 10, 2, 4, 8, 128)), shaped((5, 8, 128), jnp.int32)),
         in_specs=[ANY, ANY],
         out_specs=(ANY, ANY),
-        scratch_shapes=[pltpu.SemaphoreType.DMA((10,)), pltpu.SemaphoreType.DMA((10,))],
+        scratch_shapes=[
+            pltpu.VMEM((10, 2, 4, 8, 128), F32),
+            pltpu.VMEM((10, 4, 8, 128), F32),
+            pltpu.SemaphoreType.DMA((13,)),
+            pltpu.SemaphoreType.DMA((13,)),
+        ],
         compiler_params=params(collective_id=0, has_side_effects=True),
         name="deposit",
     )(dens, anchors)
@@ -657,8 +703,9 @@
         in_specs=[VMEM] * 11,
         out_specs=(VMEM, VMEM),
         scratch_shapes=[
-            pltpu.VMEM((10, 4, 40, 128), F32),
-            pltpu.VMEM((10, 4, 8, 128), F32),
+            pltpu.VMEM((10, 4, 32, 128), F32),
+            pltpu.VMEM((2, 8, 8, 128), F32),
+            pltpu.VMEM((2, 8, 8, 128), F32),
             pltpu.VMEM((10, 4, 144, 128), F32),
             pltpu.VMEM((8, 2, 80, 128), F32),
             pltpu.VMEM((6, 48, 128), F32),
@@ -675,8 +722,8 @@
             pltpu.VMEM((slabs, 8, 128), F32),
             pltpu.VMEM((3, 8, 128), F32),
             pltpu.VMEM((tiles, 3, 8, 128), F32),
-            pltpu.SemaphoreType.DMA((28,)),
-            pltpu.SemaphoreType.DMA((28,)),
+            pltpu.SemaphoreType.DMA((39,)),
+            pltpu.SemaphoreType.DMA((39,)),
             pltpu.SemaphoreType.DMA((slabs,)),
             pltpu.SemaphoreType.DMA((slabs,)),
         ],
@@ -699,7 +746,12 @@
         out_shape=shaped((4, 8, 2, 4, 8, 128)),
         in_specs=[ANY],
         out_specs=ANY,
-        scratch_shapes=[pltpu.SemaphoreType.DMA((4,)), pltpu.SemaphoreType.DMA((4,))],
+        scratch_shapes=[
+            pltpu.VMEM((8, 2, 4, 8, 128), F32),
+            pltpu.VMEM((8, 4, 8, 128), F32),
+            pltpu.SemaphoreType.DMA((7,)),
+            pltpu.SemaphoreType.DMA((7,)),
+        ],
         compiler_params=params(collective_id=2, has_side_effects=True),
         name="send_back",
     )(windows)

time: 148 us -> 132 us (0.89)
  Pallas kernels: 142 us -> 126 us
    pallas_call x1, Pallas kernels: 71 us -> 54.1 us  [per_device(): pl.pallas_call(cycle_kernel, out_shape=(shaped((4, 8, 128, 128)), shaped(...]
    pallas_call x1, Pallas kernels: 22.7 us -> 27.8 us  [per_device(): pl.pallas_call(deposit_kernel, out_shape=(shaped((5, 10, 2, 4, 8, 128)),...]
    pallas_call x1, Pallas kernels: 26.8 us -> 22 us  [per_device(): pl.pallas_call(return_kernel, out_shape=shaped((4, 8, 2, 4, 8, 128)), in_...]
where the time goes in v2:
time: 132 us
  Pallas kernels  126 us (95%)
  local copies, waits for them, and re-layouts  3.84 us (3%)
  other arithmetic  1.35 us (1%)
    pallas_call x1, Pallas kernels, per_device(): pl.pallas_call(cycle_kernel, out_shape=(shaped((4, 8, 128, 128)), shaped(...  54.1 us
    pallas_call x1, Pallas kernels, per_device(): pl.pallas_call(deposit_kernel, out_shape=(shaped((5, 10, 2, 4, 8, 128)),...  27.8 us
    pallas_call x1, Pallas kernels, per_device(): pl.pallas_call(return_kernel, out_shape=shaped((4, 8, 2, 4, 8, 128)), in_...  22 us
    pallas_call x1, Pallas kernels, per_device(): pl.pallas_call(density_kernel, out_shape=shaped((40, 2, 4, 8, 128)), in_s...  6.22 us
    pallas_call x1, Pallas kernels, per_device(): pl.pallas_call(window_kernel, out_shape=(shaped((4, 8, 128, 128)), shaped...  6.2 us
    pallas_call x1, Pallas kernels, per_device(): pl.pallas_call(accumulate_kernel, out_shape=shaped((10, 4, 160, 128)), in...  5.71 us
    pallas_call x1, Pallas kernels, per_device(): pl.pallas_call(project_kernel, out_shape=shaped((2, 32, 128)), in_specs=[...  3.45 us

profile of v2, /device:TPU:7, one launch (start us, length us, event | category | flops | bytes accessed | tf_op | source)
XLA Modules:
  0.0 131.6 jit_solution(2120570451122616053)
XLA Ops:
  0.7 0.9 pad_add_fusion
  1.6 0.9 copy.19
  2.5 0.5 multiply_bitcast_fusion
  2.9 1.5 %reshape.19 = bf16[2,256,64]{1,2,0:T(8,128)(2,1)S(1)} reshape(bf16[2,8,4,8,8,8]{3,2,1,5,4,0:T(4,128)(2,1)S(1)} %multiply_bitcast_fusion) | data formatting | bytes 131072 | tf_op jit(solution)/shard_map/reshape | solution.py:657
  4.4 0.1 copy.20.mix_ref
  4.5 0.5 copy_bitcast_fusion
  5.0 0.2 copy-done.10
  5.2 6.2 %density.1.src_ref.own_ref = f32[40,2,4,8,128]{4,3,2,1,0:T(8,128)S(1)} custom-call(s32[2]{0:T(128)S(1)} %copy-done.10, bf16[2,8,256,128]{3,2,1,0:T(8,128)(2,1)S(1)} %get-tuple-element.15.occ_ref, bf16[2,8,256,128]{3,2,1,0:T(8,128)(2,1)S(1)} %get-tuple-element.14.vir_ref, bf16[2,256,64]{2,1,0:T(8,128)(2,1)S(1)} %copy.20.mix_ref), custom_call_target="tpu_custom_call" | custom-call | tf_op jit(solution)/shard_map/density/pallas_call | solution.py:664
  11.4 27.8 %deposit.1 = (f32[5,10,2,4,8,128]{5,4,3,2,1,0:T(8,128)S(1)}, s32[5,8,128]{2,1,0:T(8,128)S(1)}) custom-call(f32[40,2,4,8,128]{4,3,2,1,0:T(8,128)S(1)} %density.1.src_ref.own_ref, s32[8,128]{1,0:T(8,128)S(1)} %broadcast_in_dim.10.anc_ref), custom_call_target="tpu_custom_call" | custom-call | tf_op jit(solution)/shard_map/deposit/pallas_call | solution.py:673
  39.2 0.0 copy-start
  39.2 0.0 copy-start.1
  39.2 0.0 copy-start.2
  39.3 0.0 copy-start.4
  39.3 0.0 copy-start.5
  39.3 0.0 copy-start.6
  39.3 0.0 copy-start.7
  39.3 0.0 copy-start.8
  39.3 0.0 copy-start.9
  39.3 5.7 %accumulate.1.f_ref = f32[10,4,160,128]{3,2,1,0:T(8,128)S(1)} custom-call(s32[8,128]{1,0:T(8,128)S(1)} %broadcast_in_dim.10.anc_ref, s32[5,8,128]{2,1,0:T(8,128)S(1)} %get-tuple-element.8.ganc_ref, f32[40,2,4,8,128]{4,3,2,1,0:T(8,128)S(1)} %density.1.src_ref.own_ref, f32[5,10,2,4,8,128]{5,4,3,2,1,0:T(8,128)S(1)} %get-tuple-element.9.got_ref), custom_call_target="tpu_custom_call" | custom-call | tf_op jit(solution)/shard_map/accumulate/pallas_call | solution.py:688
  45.2 54.1 %cycle.1 = (f32[4,8,128,128]{3,2,1,0:T(8,128)S(1)}, f32[4,8,32,128]{3,2,1,0:T(8,128)S(1)}) custom-call(f32[10,4,160,128]{3,2,1,0:T(8,128)S(1)} %accumulate.1.f_ref, bf16[256,128]{1,0:T(8,128)(2,1)S(1)} %copy-done.9, bf16[2,128,128]{2,1,0:T(8,128)(2,1)S(1)} %copy-done.8, bf16[2,128,128]{2,1,0:T(8,128)(2,1)S(1)} %copy-done.7, bf16[128,256]{1,0:T(8,128)(2,1)S(1)} %copy-done.6, ...), custom_call_target="tpu_custom_call" | custom-call | tf_op jit(solution)/shard_map/cycle/pallas_call | solution.py:700
  99.3 6.2 %window.1 = (f32[4,8,128,128]{3,2,1,0:T(8,128)}, f32[5,8,2,4,8,128]{5,4,3,2,1,0:T(8,128)S(1)}) custom-call(s32[8,128]{1,0:T(8,128)S(1)} %broadcast_in_dim.10.anc_ref, s32[5,8,128]{2,1,0:T(8,128)S(1)} %get-tuple-element.8.ganc_ref, f32[4,8,128,128]{3,2,1,0:T(8,128)S(1)} %get-tuple-element.10.pot_ref, f32[4,8,32,128]{3,2,1,0:T(8,128)S(1)} %get-tuple-element.11.margin_ref), custom_call_target="tpu_custom_call" | custom-call | tf_op jit(solution)/shard_map/window/pallas_call | solution.py:734
  105.5 22.0 %send_back.1.got_ref = f32[4,8,2,4,8,128]{5,4,3,2,1,0:T(8,128)S(1)} custom-call(f32[5,8,2,4,8,128]{5,4,3,2,1,0:T(8,128)S(1)} %get-tuple-element.13.src_ref.own_ref), custom_call_target="tpu_custom_call" | custom-call | tf_op jit(solution)/shard_map/send_back/pallas_call | solution.py:744
  127.5 3.4 %project.1 = f32[2,32,128]{2,1,0:T(8,128)S(1)} custom-call(s32[2]{0:T(128)S(1)} %copy-done.10, bf16[2,8,256,128]{3,2,1,0:T(8,128)(2,1)S(1)} %get-tuple-element.15.occ_ref, bf16[2,8,256,128]{3,2,1,0:T(8,128)(2,1)S(1)} %get-tuple-element.14.vir_ref, f32[5,8,2,4,8,128]{5,4,3,2,1,0:T(8,128)S(1)} %get-tuple-element.13.src_ref.own_ref, ...), custom_call_target="tpu_custom_call" | custom-call | tf_op jit(solution)/shard_map/project/pallas_call | solution.py:759
  131.0 0.6 slice_bitcast_fusion
  (19 shorter events, 0.0 us)
Async XLA Ops:
  0.6 3.9 %copy-start.11 = (bf16[2,8,32768]{2,1,0:T(8,128)(2,1)S(1)}, bf16[2,8,32768]{2,1,0:T(8,128)(2,1)}, u32[]{:S(2)}) copy-start(bf16[2,8,32768]{2,1,0:T(8,128)(2,1)} %param.17) | copy-start | bytes 3145732
  0.6 3.9 %copy-start.12 = (bf16[2,8,32768]{2,1,0:T(8,128)(2,1)S(1)}, bf16[2,8,32768]{2,1,0:T(8,128)(2,1)}, u32[]{:S(2)}) copy-start(bf16[2,8,32768]{2,1,0:T(8,128)(2,1)} %param.16) | copy-start | bytes 3145732
  4.5 0.7 copy-start.10
  39.2 5.8 %copy-start = (f32[4,256,128]{2,1,0:T(8,128)S(1)}, f32[4,256,128]{2,1,0:T(8,128)}, u32[]{:S(2)}) copy-start(f32[4,256,128]{2,1,0:T(8,128)} %constant.31.clone.inv_ref) | copy-start | bytes 1572868
  39.2 5.8 %copy-start.1 = (f32[256,256]{1,0:T(8,128)S(1)}, f32[256,256]{1,0:T(8,128)}, u32[]{:S(2)}) copy-start(f32[256,256]{1,0:T(8,128)} %constant.30.clone.kx_ref) | copy-start | bytes 786436
  39.2 5.8 %copy-start.2 = (f32[4,64,128]{2,1,0:T(8,128)S(1)}, f32[4,64,128]{2,1,0:T(8,128)}, u32[]{:S(2)}) copy-start(f32[4,64,128]{2,1,0:T(8,128)} %constant.28.clone.fy_ref) | copy-start | bytes 393220
  39.3 5.8 %copy-start.3 = (f32[4,48,128]{2,1,0:T(8,128)S(1)}, f32[4,48,128]{2,1,0:T(8,128)}, u32[]{:S(2)}) copy-start(f32[4,48,128]{2,1,0:T(8,128)} %constant.29.clone.by_ref) | copy-start | bytes 294916
  39.3 5.8 %copy-start.4 = (f32[128,128]{1,0:T(8,128)S(1)}, f32[128,128]{1,0:T(8,128)}, u32[]{:S(2)}) copy-start(f32[128,128]{1,0:T(8,128)} %constant.27.clone.bz_ref) | copy-start | bytes 196612
  39.3 5.8 %copy-start.5 = (f32[128,128]{1,0:T(8,128)S(1)}, f32[128,128]{1,0:T(8,128)}, u32[]{:S(2)}) copy-start(f32[128,128]{1,0:T(8,128)} %constant.26.clone.fz_ref) | copy-start | bytes 196612
  39.3 5.8 %copy-start.6 = (bf16[128,256]{1,0:T(8,128)(2,1)S(1)}, bf16[128,256]{1,0:T(8,128)(2,1)}, u32[]{:S(2)}) copy-start(bf16[128,256]{1,0:T(8,128)(2,1)} %constant.25.clone.p0_ref) | copy-start | bytes 196612
  39.3 5.8 %copy-start.7 = (bf16[2,128,128]{2,1,0:T(8,128)(2,1)S(1)}, bf16[2,128,128]{2,1,0:T(8,128)(2,1)}, u32[]{:S(2)}) copy-start(bf16[2,128,128]{2,1,0:T(8,128)(2,1)} %constant.24.clone.p1_ref) | copy-start | bytes 196612
  39.3 5.8 %copy-start.8 = (bf16[2,128,128]{2,1,0:T(8,128)(2,1)S(1)}, bf16[2,128,128]{2,1,0:T(8,128)(2,1)}, u32[]{:S(2)}) copy-start(bf16[2,128,128]{2,1,0:T(8,128)(2,1)} %constant.23.clone.r1_ref) | copy-start | bytes 196612
  39.3 5.8 %copy-start.9 = (bf16[256,128]{1,0:T(8,128)(2,1)S(1)}, bf16[256,128]{1,0:T(8,128)(2,1)}, u32[]{:S(2)}) copy-start(bf16[256,128]{1,0:T(8,128)(2,1)} %constant.22.clone.r0_ref) | copy-start | bytes 196612

commit v3 on v1

v3 whole, which is shorter than its diff:
```python
import functools

import jax
import jax.numpy as jnp
import numpy as np
from jax import lax
from jax.experimental import pallas as pl
from jax.experimental.pallas import tpu as pltpu
from jax.sharding import PartitionSpec as P

BOX = 32
TRIALS = 4
CX = 8
CY = 128
NZ = 128
SCREEN = 0.05
DAMPING = 2.0 / 3.0
MESH = pl.DeviceIdType.MESH
F32 = jnp.float32
BF16 = jnp.bfloat16
HIGH = lax.Precision.HIGHEST
VMEM = pl.BlockSpec(memory_space=pltpu.VMEM)
SMEM = pl.BlockSpec(memory_space=pltpu.SMEM)
ANY = pl.BlockSpec(memory_space=pl.ANY)


def center_of(level):
    spacing = 2.0**level
    return 6.0 / spacing**2 + SCREEN**2


def split2(x):
    hi = x.astype(BF16)
    lo = (x - hi.astype(F32)).astype(BF16)
    return hi, lo


def dot(a, b):
    return jnp.dot(a, b, preferred_element_type=F32)


def dot_right(x, w):
    hi, lo = split2(x)
    return dot(hi, w) + dot(lo, w)


def dot_left(w, x):
    hi, lo = split2(x)
    return dot(w, hi) + dot(w, lo)


def dot_high(a, b):
    return jnp.dot(a, b, preferred_element_type=F32, precision=HIGH)


def z_beside(x, n):
    if n == 128:
        return pltpu.roll(x, 1, 1) + pltpu.roll(x, 127, 1)
    lane = lax.broadcasted_iota(jnp.int32, x.shape, 1) % n
    below = jnp.where(lane == 0, pltpu.roll(x, 129 - n, 1), pltpu.roll(x, 1, 1))
    above = jnp.where(lane == n - 1, pltpu.roll(x, n - 1, 1), pltpu.roll(x, 127, 1))
    return below + above


def hartley_np(count):
    index = np.arange(count)
    angle = 2.0 * np.pi / count * ((index[:, None] * index[None, :]) % count)
    return (np.cos(angle) + np.sin(angle)) / np.sqrt(count)


def eigen_np(count, spacing):
    return (2.0 - 2.0 * np.cos(2.0 * np.pi / count * np.arange(count))) / (spacing * spacing)


@functools.lru_cache(None)
def tables(slabs, tiles):
    out = {}
    r0 = np.zeros((2, 128, 2, 64))
    r1 = np.zeros((2, 2, 64, 4, 32))
    p1 = np.zeros((2, 4, 32, 2, 64))
    p0 = np.zeros((2, 64, 2, 128))
    for t in range(2):
        for z in range(128):
            r0[t, z, t, z // 2] = 0.125
            p0[t, z // 2, t, z] = 1.0
        for z in range(64):
            for p in range(2):
                r1[p, t, z, 2 * p + t, z // 2] = 0.125
                p1[p, 2 * p + t, z // 2, t, z] = 1.0
    out["r0"] = r0.reshape(256, 128)
    out["r1"] = r1.reshape(2, 128, 128)
    out["p1"] = p1.reshape(2, 128, 128)
    out["p0"] = p0.reshape(128, 256)
    hz = hartley_np(16)
    mean_z = np.zeros((32, 16))
    mean_z[np.arange(32), np.arange(32) // 2] = 1.0
    fz = np.zeros((4, 32, 128))
    bz = np.zeros((128, 4, 32))
    for t in range(4):
        fz[t, :, t * 16 : t * 16 + 16] = 0.125 * mean_z @ hz
        bz[t * 16 : t * 16 + 16, t, :] = hz @ mean_z.T
    out["fz"] = fz.reshape(128, 128)
    out["bz"] = bz.reshape(128, 128)
    size_y = 16 * tiles
    hy = hartley_np(size_y)
    mean_y = np.zeros((16, 32))
    mean_y[np.arange(32) // 2, np.arange(32)] = 1.0
    fy = np.zeros((tiles, size_y, 128))
    by = np.zeros((tiles, 48, 128))
    for q in range(tiles):
        fy[q, :, :32] = hy[:, q * 16 : q * 16 + 16] @ mean_y
        for y in range(-2, 34):
            by[q, 8 + y, :size_y] = hy[(q * 16 + y // 2) % size_y]
    out["fy"] = fy
    out["by"] = by
    out["kx"] = np.kron(hartley_np(slabs), np.eye(8))
    lam_x, lam_y, lam_z = eigen_np(slabs, 8.0), eigen_np(size_y, 8.0), eigen_np(16, 8.0)
    inv = np.zeros((tiles, slabs, 8, 2, 4, 16))
    for q in range(tiles):
        ky = lam_y[q * 16 : q * 16 + 16].reshape(2, 8)
        total = (
            SCREEN * SCREEN
            + lam_x[:, None, None, None, None]
            + ky.T[None, :, :, None, None]
            + lam_z[None, None, None, None, :]
        )
        inv[q] = np.broadcast_to(1.0 / total, (slabs, 8, 2, 4, 16))
    out["inv"] = inv.reshape(tiles, slabs * 8, 128)
    return out


class Shift:
    def __init__(self, sign, pieces, relays, send, recv, slot):
        gx, gy = lax.axis_index("gx"), lax.axis_index("gy")
        n = lax.axis_size("gx")
        place = lax.rem(gx, 4) if sign > 0 else 3 - lax.rem(gx, 4)

        def copy(src, dst, at, k):
            return pltpu.make_async_remote_copy(
                src_ref=src, dst_ref=dst, send_sem=send.at[slot + at], recv_sem=recv.at[slot + at],
                device_id=(lax.rem(gx + sign * k + n, n), gy), device_id_type=MESH,
            )

        held = len(pieces)
        count = held + len(relays)
        self.relays = []
        for r, (k, src, dst, hold, least) in enumerate(relays):
            straight = copy(src, dst, held + r, k)
            first = copy(src, hold, count + r, 4)
            second = copy(hold, dst, held + r, k - 4)
            self.relays.append((straight, first, second, place >= least))
        self.whole = [copy(src, dst, p, k) for p, (k, src, dst) in enumerate(pieces)]

    def start(self):
        for straight, first, second, bent in self.relays:
            pl.when(bent)(first.start)
        for c in self.whole:
            c.start()
        for straight, first, second, bent in self.relays:
            pl.when(jnp.logical_not(bent))(straight.start)

    def pass_on(self):
        for straight, first, second, bent in self.relays:

            def onward(first=first, second=second):
                first.wait_recv()
                second.start()

            pl.when(bent)(onward)

    def arrive(self):
        for straight, first, second, bent in self.relays:
            straight.wait_recv()
        for c in self.whole:
            c.wait_recv()

    def settle(self):
        for straight, first, second, bent in self.relays:

            def sent(first=first, second=second):
                first.wait_send()
                second.wait_send()

            pl.when(bent)(sent)
            pl.when(jnp.logical_not(bent))(straight.wait_send)
        for c in self.whole:
            c.wait_send()


def box_anchors(anc_ref, ganc_ref, sources):
    pairs = []
    for s in sources:
        for b in range(2):
            if s < 0:
                pairs.append((anc_ref[0, b], anc_ref[0, 2 + b]))
            else:
                pairs.append((ganc_ref[s, 0, b], ganc_ref[s, 0, 2 + b]))
    return pairs


def select_rows(pairs, axis):
    shape = (160, 320) if axis == 0 else (320, 160)
    row = lax.broadcasted_iota(jnp.int32, shape, axis)
    col = lax.broadcasted_iota(jnp.int32, shape, 1 - axis)
    want = 4 * (col % 8) + (col // 8) % 4
    box = col // 32
    for k, (ay, _) in enumerate(pairs):
        want = want + jnp.where(box == k, ay, 0)
    return jnp.where(row == want, 1.0, 0.0).astype(BF16)


def whole_kernel(
    ax_ref, anc_ref, ancs_ref, occ_ref, vir_ref, mix_ref,
    r0_ref, r1_ref, p1_ref, p0_ref, fz_ref, bz_ref, fy_ref, by_ref, kx_ref, inv_ref,
    out_ref, coup_ref,
    dens, src, got, ganc, sanc, sel, selt, hold1, hold2, f_ref,
    rim, sides, beyond, fp, f1p, f2p, v0, v1p, w1, v2p, w2, tmp, tmp1, qs, qr, gs, gall, us, ur,
    pot, margin, cut, win0, win1, hold3, hold4,
    send, recv, gsend, grecv, local,
):
    gx, gy = lax.axis_index("gx"), lax.axis_index("gy")
    n, m = lax.axis_size("gx"), lax.axis_size("gy")
    east, west = lax.rem(gx + 1, n), lax.rem(gx + n - 1, n)
    north, south = lax.rem(gy + 1, m), lax.rem(gy + m - 1, m)
    wins = (win0, win1)
    used = [0]

    def slots(count):
        used[0] += count
        return used[0] - count

    barrier = pltpu.get_barrier_semaphore()
    for d in range(1, m):
        pl.semaphore_signal(barrier, inc=1, device_id=(gx, lax.rem(gy + d, m)), device_id_type=MESH)
    for x in (east, west):
        for y in (north, south):
            pl.semaphore_signal(barrier, inc=1, device_id=(x, y), device_id_type=MESH)

    def greet(d, carry):
        pl.semaphore_signal(barrier, inc=1, device_id=(lax.rem(gx + d, n), gy), device_id_type=MESH)
        return carry

    lax.fori_loop(1, n, greet, 0)

    def copy(src_ref, dst_ref, x, y):
        slot = slots(1)
        return pltpu.make_async_remote_copy(
            src_ref=src_ref, dst_ref=dst_ref, send_sem=send.at[slot], recv_sem=recv.at[slot],
            device_id=(x, y), device_id_type=MESH,
        )

    unsent = []

    for b in range(2):
        for x in range(8):
            dens[b, x] = jnp.zeros((2, 8, 128), F32)
            dens[b, 40 + x] = jnp.zeros((2, 8, 128), F32)

    def density(p):
        for b in range(2):
            weights = mix_ref[b, p]

            def step(s, carry, b=b, weights=weights):
                rows = pl.ds(pl.multiple_of(s * 16, 16), 16)
                vir = vir_ref[b, :, rows, :].astype(F32)
                occ = occ_ref[b, :, rows, :].astype(F32)
                parts = [vir[:, 8 * h : 8 * h + 8].reshape(64, 128) for h in range(2)]
                mixed = dot(weights, jnp.concatenate(parts, axis=1).astype(BF16))
                mixed = mixed.reshape(8, 2, 8, 256)
                for h in range(2):
                    part = mixed[..., 128 * h : 128 * h + 128]
                    dens[b, 8 + 2 * s + h] = jnp.sum(occ[:, None, 8 * h : 8 * h + 8] * part, axis=0)
                return carry

            lax.fori_loop(0, 16, step, 0)

        def place(x, carry):
            for b in range(2):
                src[p, x, b] = dens[b, x + 8 - ax_ref[b]]
            return carry

        lax.fori_loop(0, 40, place, 0)

    def deposit(p):
        s, g = src.at[p], got.at[p]
        pieces = [
            (4, s.at[pl.ds(31, 8)], g.at[3, pl.ds(0, 8)]),
            (3, s.at[pl.ds(23, 10)], g.at[2]),
            (2, s.at[pl.ds(15, 10), 0], g.at[1, :, 0]),
            (-1, s.at[pl.ds(0, 1)], g.at[4, pl.ds(9, 1)]),
        ]
        relays = [
            (1, s.at[pl.ds(7, 10)], g.at[0], hold1.at[p], 3),
            (2, s.at[pl.ds(15, 10), 1], g.at[1, :, 1], hold2.at[p], 2),
        ]
        return Shift(1, pieces, relays, send, recv, slots(8))

    density(0)
    pl.semaphore_wait(barrier, m - 1 + 4 + n - 1)
    words = [copy(ancs_ref, ganc.at[s], lax.rem(gx + k + n, n), gy) for s, k in enumerate((1, 2, 3, 4, -1))]
    moves = [deposit(0), deposit(1)]
    moves[0].start()
    for c in words:
        c.start()
    density(1)
    moves[1].start()
    moves[0].pass_on()
    for c in words:
        c.wait()
    read = pltpu.make_async_copy(ganc, sanc, local.at[0])
    read.start()
    read.wait()
    usual = box_anchors(anc_ref, sanc, [-1, 0, 1, 2, 3])
    last = box_anchors(anc_ref, sanc, [-1, 0, 1, 2, 4])
    sel[0] = select_rows(usual, 0)
    sel[1] = select_rows(last, 0)
    selt[...] = select_rows(usual, 1)
    lane = lax.broadcasted_iota(jnp.int32, (8, 128), 1)
    blank = jnp.zeros((8, 128), F32)

    def plane(p, e, own, takes, edge):
        pairs = last if edge else usual
        loads = []
        for s in range(5):
            for b in range(2):
                if s == 0:
                    loads.append((lambda t, b=b: src[p, e - 1, b, t]) if own else None)
                elif s == 4 and edge:
                    loads.append(lambda t, b=b: got[p, 4, 9, b, t])
                elif s in takes:
                    loads.append(lambda t, s=s, b=b: got[p, s - 1, e, b, t])
                else:
                    loads.append(None)
        masks = [(lane >= az) & (lane < az + 32) for _, az in pairs]
        columns = []
        for t in range(2):
            rows = []
            for k, load in enumerate(loads):
                if load is None:
                    rows += [blank] * 4
                    continue
                value = load(t)
                for j in range(4):
                    moved = pltpu.roll(value, lax.rem(pairs[k][1] + 128 - 32 * j, 128), 1)
                    rows.append(jnp.where(masks[k], moved, 0.0))
            columns.append(jnp.concatenate(rows, axis=0))
        placed = dot_left(sel[1 if edge else 0], jnp.concatenate(columns, axis=1))
        f_ref[p, e, 0] = placed[:, :128]
        f_ref[p, e, 1] = placed[:, 128:]

    def accumulate(p):
        plane(p, 0, False, (1, 2, 3, 4), False)

        def step(e, carry):
            plane(p, e, True, (1, 2, 3, 4), False)
            return carry

        lax.fori_loop(1, 8, step, 0)
        plane(p, 8, True, (1, 2, 3), False)
        plane(p, 9, True, (1, 2, 3), True)

    def send_rim(p):
        copies = [copy(f_ref.at[p, :, :, pl.ds(128, 32), :], rim.at[p], gx, north)]
        copies[0].start()

        def edge(e, carry):
            for t in range(2):
                sides[p, 0, e, t : t + 1] = f_ref[p, e + 1, t, 127:128]
                sides[p, 1, e, t : t + 1] = f_ref[p, e + 1, t, 0:1]
            return carry

        lax.fori_loop(0, 8, edge, 0)
        copies += [
            copy(sides.at[p, 0], beyond.at[p, 0], gx, north),
            copy(sides.at[p, 1], beyond.at[p, 1], gx, south),
        ]
        for c in copies[1:]:
            c.start()

        def early(e, carry):
            for t in range(2):
                fp[e, 2 * p + t, 40:136] = f_ref[p, e, t, 32:128]
            return carry

        lax.fori_loop(0, 10, early, 0)
        return copies

    def join_rim(p, copies):
        for c in copies:
            c.wait_recv()
        unsent.extend(copies)

        def join(e, carry):
            for t in range(2):
                fp[e, 2 * p + t, 8:40] = f_ref[p, e, t, 0:32] + rim[p, e, t]
            return carry

        def rims(e, carry):
            for t in range(2):
                fp[e, 2 * p + t, 7:8] = beyond[p, 0, e - 1, t : t + 1]
                fp[e, 2 * p + t, 136:137] = f_ref[p, e, t, 128:129] + beyond[p, 1, e - 1, t : t + 1]
            return carry

        lax.fori_loop(1, 9, rims, 0)
        lax.fori_loop(0, 10, join, 0)

    def down0(p):
        scale = DAMPING / center_of(0)

        def step(xc, carry):
            halves = []
            for t in (2 * p, 2 * p + 1):
                total = None
                for x in range(2):
                    e = 2 * xc + 1 + x
                    mid = fp[e, t, 8:136]
                    beside = fp[e, t, 7:135] + fp[e, t, 9:137] + fp[e - 1, t, 8:136] + fp[e + 1, t, 8:136]
                    beside = beside + z_beside(mid, 128)
                    res = (1.0 - DAMPING) * mid + scale * beside
                    total = res if total is None else total + res
                tmp[0:128, :] = total
                halves.append(tmp[pl.ds(0, 64, stride=2), :] + tmp[pl.ds(1, 64, stride=2), :])
            f1p[p, 2 + xc, 8:72] = dot_right(jnp.concatenate(halves, axis=1), r0_ref[...])
            return carry

        lax.fori_loop(0, 4, step, 0)

    def swap(buf, a, c):
        def part(x0, nx, y0, ny):
            return buf.at[pl.ds(x0, nx), pl.ds(y0, ny)]

        near = [
            copy(part(a + 1, 1, 8, c), part(1, 1, 8, c), east, gy),
            copy(part(2, 1, 8, c), part(a + 2, 1, 8, c), west, gy),
            copy(part(2, a, c, 8), part(2, a, 0, 8), gx, north),
            copy(part(2, a, 8, 8), part(2, a, c + 8, 8), gx, south),
        ]
        far = [
            copy(part(a, 1, 8, c), part(0, 1, 8, c), east, gy),
            copy(part(3, 1, 8, c), part(a + 3, 1, 8, c), west, gy),
            copy(part(a, 2, c, 8), part(0, 2, 0, 8), east, north),
            copy(part(a, 2, 8, 8), part(0, 2, c + 8, 8), east, south),
            copy(part(2, 2, c, 8), part(a + 2, 2, 0, 8), west, north),
            copy(part(2, 2, 8, 8), part(a + 2, 2, c + 8, 8), west, south),
        ]
        for one in near + far:
            one.start()
        unsent.extend(near + far)
        return near, far

    moves[0].arrive()
    accumulate(0)
    rims0 = send_rim(0)
    moves[1].pass_on()
    join_rim(0, rims0)
    down0(0)
    near0, far0 = swap(f1p.at[0], 4, 64)
    moves[1].arrive()
    accumulate(1)
    rims1 = send_rim(1)
    join_rim(1, rims1)
    down0(1)
    near1, far1 = swap(f1p.at[1], 4, 64)

    def down1(p, xc):
        scale = DAMPING / center_of(1) / 4.0
        both = None
        for x in range(2):
            e = 2 + 2 * xc + x
            mid = f1p[p, e, 8:72]
            beside = f1p[p, e, 7:71] + f1p[p, e, 9:73] + f1p[p, e - 1, 8:72] + f1p[p, e + 1, 8:72]
            beside = beside + z_beside(mid, 64)
            res = (1.0 - DAMPING) * mid + scale * beside
            both = res if both is None else both + res
        tmp[0:64, :] = both
        pair = tmp[pl.ds(0, 32, stride=2), :] + tmp[pl.ds(1, 32, stride=2), :]
        return dot_right(pair, r1_ref[p])

    for c in near0:
        c.wait_recv()
    held = [down1(0, xc) for xc in range(2)]
    for c in near1:
        c.wait_recv()
    for xc in range(2):
        f2p[2 + xc, 8:40] = held[xc] + down1(1, xc)
    near2, far2 = swap(f2p, 2, 32)
    for c in near2:
        c.wait_recv()

    scale = DAMPING / center_of(2) / 16.0
    total = None
    for x in range(2):
        e = 2 + x
        mid = f2p[e, 8:40]
        beside = f2p[e, 7:39] + f2p[e, 9:41] + f2p[e - 1, 8:40] + f2p[e + 1, 8:40]
        beside = beside + z_beside(mid, 32)
        res = (1.0 - DAMPING) * mid + scale * beside
        total = res if total is None else total + res
    modes = dot_high(total, fz_ref[...])
    modes = jnp.concatenate([modes, jnp.zeros((96, 128), F32)], axis=0)
    modes = dot_high(fy_ref[gy], modes)
    for q in range(m):
        qs[q] = modes[16 * q : 16 * q + 8] + pltpu.roll(modes[16 * q + 8 : 16 * q + 16], 64, 1)
    copies = []
    for d in range(1, m):
        to = lax.rem(gy + d, m)
        copies.append(copy(qs.at[to], qr.at[d - 1], gx, to))
    for c in copies:
        c.start()
    unsent.extend(copies)
    mine = qs[gy]
    for d, c in enumerate(copies):
        c.wait_recv()
        mine = mine + qr[d]
    gs[...] = mine

    def shout(d):
        return pltpu.make_async_remote_copy(
            src_ref=gs, dst_ref=gall.at[gx], send_sem=gsend.at[d], recv_sem=grecv.at[d],
            device_id=(lax.rem(gx + d, n), gy), device_id_type=MESH,
        )

    def begin(d, carry):
        shout(d).start()
        return carry

    def end(d, carry):
        shout(d).wait()
        return carry

    lax.fori_loop(1, n, begin, 0)
    gall[gx] = mine
    lax.fori_loop(1, n, end, 0)
    spectrum = dot_high(kx_ref[...], gall[...].reshape(8 * n, 128)) * inv_ref[gy]
    for s, x in enumerate((west, gx, east)):
        us[s] = dot_high(kx_ref[pl.ds(pl.multiple_of(8 * x, 8), 8), :], spectrum)

    copies = []
    for d in range(1, m):
        to = lax.rem(gy + d, m)
        copies.append(copy(us, ur.at[gy], gx, to))
    for c in copies:
        c.start()
    unsent.extend(copies)
    ur[gy] = us[...]
    for c in copies:
        c.wait_recv()

    for c in far2:
        c.wait_recv()
    scale = DAMPING / center_of(2)
    for s in range(3):
        rows = []
        for q in range(m):
            half = ur[q, s]
            rows += [half, pltpu.roll(half, 64, 1)]
        if m < 8:
            rows.append(jnp.zeros((128 - 16 * m, 128), F32))
        ahead = dot_high(by_ref[gy], jnp.concatenate(rows, axis=0))
        ahead = dot_high(ahead, bz_ref[...])
        for x in range(2):
            v2p[2 * s + x] = scale * f2p[2 * s + x] + ahead
    for e in range(1, 5):
        mid = v2p[e]
        beside = v2p[e - 1] + v2p[e + 1] + pltpu.roll(mid, 1, 0) + pltpu.roll(mid, 47, 0)
        beside = beside + z_beside(mid, 32)
        w2[e - 1] = (1.0 - DAMPING) * mid + scale * f2p[e] + (scale / 16.0) * beside

    def rise1(p):
        scale = DAMPING / center_of(1)
        for e in range(4):
            wide = dot_right(w2[e, 4:44], p1_ref[p])
            tmp[pl.ds(0, 40, stride=2), :] = wide
            tmp[pl.ds(1, 40, stride=2), :] = wide
            for x in range(2):
                v1p[2 * e + x] = scale * f1p[p, 2 * e + x] + tmp[0:80, :]

        def step(e, carry):
            mid = v1p[e]
            beside = v1p[e - 1] + v1p[e + 1] + pltpu.roll(mid, 1, 0) + pltpu.roll(mid, 79, 0)
            beside = beside + z_beside(mid, 64)
            w1[e - 1] = (1.0 - DAMPING) * mid + scale * f1p[p, e] + (scale / 4.0) * beside
            return carry

        lax.fori_loop(1, 7, step, 0)

    def rise0(p):
        scale = DAMPING / center_of(0)

        def widen(i):
            wide = dot_right(w1[i, 4:76], p0_ref[...])
            for t in range(2):
                tmp1[t, pl.ds(0, 72, stride=2), :] = wide[:, 128 * t : 128 * t + 128]
                tmp1[t, pl.ds(1, 72, stride=2), :] = wide[:, 128 * t : 128 * t + 128]

        for i, e in ((0, 0), (5, 9)):
            widen(i)
            for t in range(2):
                v0[e, t] = scale * fp[e, 2 * p + t] + tmp1[t]

        def lift(i, carry):
            widen(i)
            for x in range(2):
                for t in range(2):
                    v0[2 * i - 1 + x, t] = scale * fp[2 * i - 1 + x, 2 * p + t] + tmp1[t]
            return carry

        lax.fori_loop(1, 5, lift, 0)

        def step(e, carry):
            for t in range(2):
                mid = v0[e, t, 8:136]
                beside = v0[e, t, 7:135] + v0[e, t, 9:137] + v0[e - 1, t, 8:136] + v0[e + 1, t, 8:136]
                beside = beside + z_beside(mid, 128)
                pot[2 * p + t, e - 1] = (1.0 - DAMPING) * mid + scale * (fp[e, 2 * p + t, 8:136] + beside)
            return carry

        lax.fori_loop(1, 9, step, 0)

    def send_margin(p):
        pair = pl.ds(2 * p, 2)
        c = copy(pot.at[pair, :, pl.ds(0, 32), :], margin.at[pair], gx, south)
        c.start()
        unsent.append(c)
        keep = pltpu.make_async_copy(pot.at[pair], out_ref.at[pair], local.at[1 + p])
        keep.start()
        return c, keep

    group = lax.broadcasted_iota(jnp.int32, (8, 128), 1) // 32

    def windows(p):
        def step(x, carry):
            columns = [
                jnp.concatenate([pot[2 * p + t, x], margin[2 * p + t, x]], axis=0) for t in range(2)
            ]
            taken = dot_left(selt[...], jnp.concatenate(columns, axis=1))
            for t in range(2):
                for k in range(10):
                    total = None
                    for j in range(4):
                        piece = taken[32 * k + 8 * j : 32 * k + 8 * j + 8, 128 * t : 128 * t + 128]
                        piece = pltpu.roll(piece, lax.rem(128 + 32 * j - usual[k][1], 128), 1)
                        total = piece if total is None else jnp.where(group == j, piece, total)
                    if k < 2:
                        wins[p][x, k, t] = total
                    else:
                        cut[p, k // 2 - 1, x, k % 2, t] = total
            return carry

        lax.fori_loop(0, 8, step, 0)

    def give_back(p):
        c, w = cut.at[p], wins[p]
        pieces = [
            (4, c.at[3], w.at[pl.ds(32, 8)]),
            (3, c.at[2], w.at[pl.ds(24, 8)]),
            (2, c.at[1, :, 0], w.at[pl.ds(16, 8), 0]),
        ]
        relays = [
            (1, c.at[0], w.at[pl.ds(8, 8)], hold3.at[p], 3),
            (2, c.at[1, :, 1], w.at[pl.ds(16, 8), 1], hold4.at[p], 2),
        ]
        return Shift(-1, pieces, relays, send, recv, slots(7))

    def project(p):
        for b in range(2):

            def step(s, total, b=b):
                left, right = [], []
                for h in range(4):
                    rows = pl.ds(pl.multiple_of(s * 64 + 16 * h, 16), 16)
                    occ = occ_ref[b, :, rows, :].astype(F32)
                    vir = vir_ref[b, :, rows, :].astype(F32)
                    for g in range(2):
                        cells = wins[p][ax_ref[b] + s * 8 + 2 * h + g, b]
                        weighted = occ[None, :, 8 * g : 8 * g + 8] * cells[:, None]
                        left.append(weighted.reshape(128, 128).astype(BF16))
                        right.append(vir[:, 8 * g : 8 * g + 8].reshape(64, 128).astype(BF16))
                left, right = jnp.concatenate(left, axis=1), jnp.concatenate(right, axis=1)
                return total + lax.dot_general(
                    left, right, (((1,), (1,)), ((), ())), preferred_element_type=F32
                )

            total = lax.fori_loop(0, 4, step, jnp.zeros((128, 64), F32))
            row = lax.broadcasted_iota(jnp.int32, (128, 64), 0) % 8
            col = lax.broadcasted_iota(jnp.int32, (128, 64), 1) % 8
            total = jnp.where(row == col, total, 0.0)
            total = jnp.sum(total.reshape(16, 8, 64), axis=1)
            col = lax.broadcasted_iota(jnp.int32, (64, 128), 1)
            row = lax.broadcasted_iota(jnp.int32, (64, 128), 0) // 8
            pick = jnp.where(row == col, float(BOX) ** (-1.5), 0.0)
            coup_ref[b, 16 * p : 16 * p + 16] = dot_high(total, pick)

    for c in far0:
        c.wait_recv()
    rise1(0)
    rise0(0)
    edge0, keep0 = send_margin(0)
    for c in far1:
        c.wait_recv()
    rise1(1)
    rise0(1)
    edge1, keep1 = send_margin(1)
    backs = [give_back(0), give_back(1)]
    edge0.wait_recv()
    windows(0)
    backs[0].start()
    edge1.wait_recv()
    windows(1)
    backs[1].start()
    backs[0].pass_on()
    backs[0].arrive()
    backs[1].pass_on()
    project(0)
    backs[1].arrive()
    project(1)
    keep0.wait()
    keep1.wait()
    for c in unsent:
        c.wait_send()
    for c in moves + backs:
        c.settle()


def params(**more):
    return pltpu.CompilerParams(vmem_limit_bytes=40 * 1024 * 1024, **more)


def shaped(shape, dtype=F32):
    return jax.ShapeDtypeStruct(shape, dtype)


def per_device(slabs, tiles, occupied, virtual, trials, anchor_x, anchor_y, anchor_z):
    occ = occupied.reshape(2, 8, 256, 128)
    vir = virtual.reshape(2, 8, 256, 128)
    mix = jnp.einsum("bpsia,mn->bpisman", trials.reshape(2, 2, 2, 8, 8), jnp.eye(8, dtype=BF16))
    mix = mix.reshape(2, 2, 128, 64)
    anchors = jnp.concatenate([anchor_y, anchor_z, jnp.zeros((124,), jnp.int32)])
    anchors = jnp.broadcast_to(anchors[None], (8, 128))
    tab = tables(slabs, tiles)
    exact = [jnp.asarray(tab[k], BF16) for k in ("r0", "r1", "p1", "p0")]
    wide = [jnp.asarray(tab[k], F32) for k in ("fz", "bz", "fy", "by", "kx", "inv")]
    potential, coupling = pl.pallas_call(
        whole_kernel,
        out_shape=(shaped((4, 8, 128, 128)), shaped((2, 32, 128))),
        in_specs=[SMEM, SMEM] + [VMEM] * 14,
        out_specs=(ANY, VMEM),
        scratch_shapes=[
            pltpu.VMEM((2, 48, 2, 8, 128), F32),
            pltpu.VMEM((2, 40, 2, 2, 8, 128), F32),
            pltpu.VMEM((2, 5, 10, 2, 2, 8, 128), F32),
            pltpu.VMEM((5, 8, 128), jnp.int32),
            pltpu.SMEM((5, 8, 128), jnp.int32),
            pltpu.VMEM((2, 160, 320), BF16),
            pltpu.VMEM((320, 160), BF16),
            pltpu.VMEM((2, 10, 2, 2, 8, 128), F32),
            pltpu.VMEM((2, 10, 2, 8, 128), F32),
            pltpu.VMEM((2, 10, 2, 160, 128), F32),
            pltpu.VMEM((2, 10, 2, 32, 128), F32),
            pltpu.VMEM((2, 2, 8, 8, 128), F32),
            pltpu.VMEM((2, 2, 8, 8, 128), F32),
            pltpu.VMEM((10, 4, 144, 128), F32),
            pltpu.VMEM((2, 8, 80, 128), F32),
            pltpu.VMEM((6, 48, 128), F32),
            pltpu.VMEM((10, 2, 144, 128), F32),
            pltpu.VMEM((8, 80, 128), F32),
            pltpu.VMEM((6, 80, 128), F32),
            pltpu.VMEM((6, 48, 128), F32),
            pltpu.VMEM((4, 48, 128), F32),
            pltpu.VMEM((144, 128), F32),
            pltpu.VMEM((2, 144, 128), F32),
            pltpu.VMEM((tiles, 8, 128), F32),
            pltpu.VMEM((tiles, 8, 128), F32),
            pltpu.VMEM((8, 128), F32),
            pltpu.VMEM((slabs, 8, 128), F32),
            pltpu.VMEM((3, 8, 128), F32),
            pltpu.VMEM((tiles, 3, 8, 128), F32),
            pltpu.VMEM((4, 8, 128, 128), F32),
            pltpu.VMEM((4, 8, 32, 128), F32),
            pltpu.VMEM((2, 4, 8, 2, 2, 8, 128), F32),
            pltpu.VMEM((40, 2, 2, 8, 128), F32),
            pltpu.VMEM((40, 2, 2, 8, 128), F32),
            pltpu.VMEM((2, 8, 2, 2, 8, 128), F32),
            pltpu.VMEM((2, 8, 2, 8, 128), F32),
            pltpu.SemaphoreType.DMA((96,)),
            pltpu.SemaphoreType.DMA((96,)),
            pltpu.SemaphoreType.DMA((slabs,)),
            pltpu.SemaphoreType.DMA((slabs,)),
            pltpu.SemaphoreType.DMA((3,)),
        ],
        compiler_params=params(collective_id=0, has_side_effects=True),
        name="whole",
    )(anchor_x, anchors, anchors, occ, vir, mix, *exact, *wide)
    return potential, coupling[:, :, :8].reshape(2, 4, 8, 8)


def solution(mesh):
    placed = (
        P(("gx", "gy"), None, None),
        P(("gx", "gy"), None, None),
        P(("gx", "gy"), None, None, None),
        P(("gx", "gy")),
        P(("gx", "gy")),
        P(("gx", "gy")),
    )
    return jax.shard_map(
        functools.partial(per_device, mesh.shape["gx"], mesh.shape["gy"]),
        mesh=mesh,
        in_specs=placed,
        out_specs=(P(None, "gx", "gy", None), P(("gx", "gy"), None, None, None)),
        check_vma=False,
    )
```

time: 148 us -> 118 us (0.80)
  the two profiles are of different devices: /device:TPU:7 before, /device:TPU:13 now
where the time goes in v3:
time: 118 us
  Pallas kernels  110 us (93%)
  local copies, waits for them, and re-layouts  5.36 us (5%)
  other arithmetic  1.76 us (1%)
    pallas_call x1, Pallas kernels, per_device(): pl.pallas_call(whole_kernel, out_shape=(shaped((4, 8, 128, 128)), shaped(...  110 us

profile of v3, /device:TPU:13, one launch (start us, length us, event | category | flops | bytes accessed | tf_op | source)
XLA Modules:
  0.0 118.1 jit_solution(9240396461088285439)
XLA Ops:
  0.7 0.9 pad_add_fusion
  1.6 1.0 copy.19
  2.6 0.9 multiply_bitcast_fusion
  3.4 1.1 reshape.23
  4.6 0.1 copy.20.mix_ref
  4.7 0.0 copy-start.1
  4.7 0.0 copy-start.2
  4.8 0.0 copy-start.3
  4.8 0.0 copy-start.4
  4.8 0.0 copy-start.5
  4.8 0.0 copy-start.6
  4.8 0.0 copy-start.8
  4.9 0.5 copy_bitcast_fusion
  5.3 0.4 copy-done
  5.8 0.1 copy-done.1
  5.8 0.0 copy-done.2
  5.9 0.0 copy-done.3
  5.9 0.0 copy-done.6
  5.9 0.0 copy-done.7
  5.9 0.0 copy-done.8
  5.9 0.0 copy-done.9
  6.0 110.2 %whole.1 = (f32[4,8,128,128]{3,2,1,0:T(8,128)S(1)}, f32[2,32,128]{2,1,0:T(8,128)S(1)}) custom-call(s32[2]{0:T(128)S(1)} %copy-done.10, s32[8,128]{1,0:T(8,128)S(1)} %broadcast_in_dim.10.anc_ref.ancs_ref, s32[8,128]{1,0:T(8,128)S(1)} %broadcast_in_dim.10.anc_ref.ancs_ref, bf16[2,8,256,128]{3,2,1,0:T(8,128)(2,1)S(1)} %get-tuple-element.7.occ_ref, ...), custom_call_target="tpu_custom_call" | custom-call | tf_op jit(solution)/shard_map/whole/pallas_call | solution.py:743
  116.2 0.6 slice_bitcast_fusion
  116.8 1.3 %copy.26 = f32[4,8,128,128]{3,2,1,0:T(8,128)} copy(f32[4,8,128,128]{3,2,1,0:T(8,128)S(1)} %get-tuple-element.10) | data formatting | bytes 4194304
  (14 shorter events, 0.0 us)
Async XLA Ops:
  0.6 4.1 %copy-start.11 = (bf16[2,8,32768]{2,1,0:T(8,128)(2,1)S(1)}, bf16[2,8,32768]{2,1,0:T(8,128)(2,1)}, u32[]{:S(2)}) copy-start(bf16[2,8,32768]{2,1,0:T(8,128)(2,1)} %param.17) | copy-start | bytes 3145732
  0.6 4.1 %copy-start.12 = (bf16[2,8,32768]{2,1,0:T(8,128)(2,1)S(1)}, bf16[2,8,32768]{2,1,0:T(8,128)(2,1)}, u32[]{:S(2)}) copy-start(bf16[2,8,32768]{2,1,0:T(8,128)(2,1)} %param.16) | copy-start | bytes 3145732
  4.7 1.0 copy-start
  4.7 1.1 copy-start.1
  4.7 1.1 copy-start.2
  4.8 1.1 copy-start.3
  4.8 1.1 copy-start.4
  4.8 1.1 copy-start.5
  4.8 1.1 copy-start.6
  4.8 1.1 copy-start.7
  4.8 1.1 copy-start.8
  4.8 1.1 copy-start.9
  4.8 1.1 copy-start.10

commit v4 on v3

--- a/solution.py
+++ b/solution.py
@@ -187,12 +187,12 @@
             c.wait_send()
 
 
-def box_anchors(anc_ref, ganc_ref, sources):
+def box_anchors(ay_ref, az_ref, ganc_ref, sources):
     pairs = []
     for s in sources:
         for b in range(2):
             if s < 0:
-                pairs.append((anc_ref[0, b], anc_ref[0, 2 + b]))
+                pairs.append((ay_ref[b], az_ref[b]))
             else:
                 pairs.append((ganc_ref[s, 0, b], ganc_ref[s, 0, 2 + b]))
     return pairs
@@ -209,13 +209,72 @@
     return jnp.where(row == want, 1.0, 0.0).astype(BF16)
 
 
+def halve(x):
+    return lax.div(x, 2)
+
+
+def one_hot(hit):
+    return jnp.where(hit, 1.0, 0.0)
+
+
+def select_coarse(pairs):
+    row = lax.broadcasted_iota(jnp.int32, (320, 96), 0)
+    col = lax.broadcasted_iota(jnp.int32, (320, 96), 1)
+    want = row % 32 + 7
+    for k, (ay, _) in enumerate(pairs):
+        want = want + jnp.where(row // 32 == k, halve(ay + 1), 0)
+    return one_hot(col == want).astype(BF16)
+
+
+def select_coarse_z(az):
+    row = lax.broadcasted_iota(jnp.int32, (256, 128), 0)
+    col = lax.broadcasted_iota(jnp.int32, (256, 128), 1)
+    want = (halve(az + 1) + 63 + col % 32) % 64
+    return one_hot((row // 64 == col // 32) & (row % 64 == want)).astype(BF16)
+
+
+def widen_rows(ay):
+    row = lax.broadcasted_iota(jnp.int32, (64, 32), 0)
+    col = lax.broadcasted_iota(jnp.int32, (64, 32), 1)
+    cell = 4 * (row % 8) + (row // 8) % 4 + ay
+    first = halve(ay + 1) - 1
+    at = [jnp.right_shift(cell + d, 1) - first for d in (0, -1, 1)]
+    beside = one_hot(col == at[1]) + one_hot(col == at[2])
+    return jnp.where(row < 32, one_hot(col == at[0]), beside).astype(BF16)
+
+
+def widen_lanes(az, j):
+    row = lax.broadcasted_iota(jnp.int32, (128, 512), 0)
+    col = lax.broadcasted_iota(jnp.int32, (128, 512), 1)
+    cell = col % 32 + az
+    first = halve(az + 1) - 1
+    same = (row // 32 == col // 128) & ((col // 32) % 4 == j)
+    at = [jnp.right_shift(cell + d, 1) - first for d in (0, -1, 1)]
+    hits = [one_hot(same & (row % 32 == a)) for a in at]
+    return hits[0].astype(BF16), (hits[1] + hits[2]).astype(BF16)
+
+
+def mixing(pair_of_trials, p):
+    row = lax.broadcasted_iota(jnp.int32, (128, 32), 0)
+    col = lax.broadcasted_iota(jnp.int32, (128, 32), 1)
+    rows = one_hot(col == (2 * p + (row // 8) % 2) * 8 + row // 16).astype(BF16)
+    taken = dot(rows, pair_of_trials).astype(BF16)
+    row = lax.broadcasted_iota(jnp.int32, (8, 64), 0)
+    col = lax.broadcasted_iota(jnp.int32, (8, 64), 1)
+    spread = dot(taken, one_hot(row == col // 8).astype(BF16))
+    row = lax.broadcasted_iota(jnp.int32, (128, 64), 0)
+    col = lax.broadcasted_iota(jnp.int32, (128, 64), 1)
+    return jnp.where(row % 8 == col % 8, spread, 0.0).astype(BF16)
+
+
 def whole_kernel(
-    ax_ref, anc_ref, ancs_ref, occ_ref, vir_ref, mix_ref,
+    ax_ref, ay_ref, az_ref, occ_ref, vir_ref, trial_ref,
     r0_ref, r1_ref, p1_ref, p0_ref, fz_ref, bz_ref, fy_ref, by_ref, kx_ref, inv_ref,
     out_ref, coup_ref,
     dens, src, got, ganc, sanc, sel, selt, hold1, hold2, f_ref,
-    rim, sides, beyond, fp, f1p, f2p, v0, v1p, w1, v2p, w2, tmp, tmp1, qs, qr, gs, gall, us, ur,
+    rim, sides, beyond, fp, f1p, f2p, v0, v1p, w1, v2p, w2, tmp, qs, qr, gs, gall, us, ur,
     pot, margin, cut, win0, win1, hold3, hold4,
+    word, mar1, selc, selz, taken, cut1, cwin, hold5, hold6, lc1, lc2, zp, zs, ub, vb,
     send, recv, gsend, grecv, local,
 ):
     gx, gy = lax.axis_index("gx"), lax.axis_index("gy")
@@ -258,7 +317,7 @@
 
     def density(p):
         for b in range(2):
-            weights = mix_ref[b, p]
+            weights = mixing(trial_ref[b], p)
 
             def step(s, carry, b=b, weights=weights):
                 rows = pl.ds(pl.multiple_of(s * 16, 16), 16)
@@ -297,7 +356,12 @@
 
     density(0)
     pl.semaphore_wait(barrier, m - 1 + 4 + n - 1)
-    words = [copy(ancs_ref, ganc.at[s], lax.rem(gx + k + n, n), gy) for s, k in enumerate((1, 2, 3, 4, -1))]
+    lane = lax.broadcasted_iota(jnp.int32, (8, 128), 1)
+    value = jnp.zeros((8, 128), jnp.int32)
+    for k, anchor in enumerate((ay_ref[0], ay_ref[1], az_ref[0], az_ref[1])):
+        value = jnp.where(lane == k, anchor, value)
+    word[...] = value
+    words = [copy(word, ganc.at[s], lax.rem(gx + k + n, n), gy) for s, k in enumerate((1, 2, 3, 4, -1))]
     moves = [deposit(0), deposit(1)]
     moves[0].start()
     for c in words:
@@ -310,12 +374,11 @@
     read = pltpu.make_async_copy(ganc, sanc, local.at[0])
     read.start()
     read.wait()
-    usual = box_anchors(anc_ref, sanc, [-1, 0, 1, 2, 3])
-    last = box_anchors(anc_ref, sanc, [-1, 0, 1, 2, 4])
+    usual = box_anchors(ay_ref, az_ref, sanc, [-1, 0, 1, 2, 3])
+    last = box_anchors(ay_ref, az_ref, sanc, [-1, 0, 1, 2, 4])
     sel[0] = select_rows(usual, 0)
     sel[1] = select_rows(last, 0)
     selt[...] = select_rows(usual, 1)
-    lane = lax.broadcasted_iota(jnp.int32, (8, 128), 1)
     blank = jnp.zeros((8, 128), F32)
 
     def plane(p, e, own, takes, edge):
@@ -417,6 +480,7 @@
                     beside = fp[e, t, 7:135] + fp[e, t, 9:137] + fp[e - 1, t, 8:136] + fp[e + 1, t, 8:136]
                     beside = beside + z_beside(mid, 128)
                     res = (1.0 - DAMPING) * mid + scale * beside
+                    pot[t, e - 1] = scale * (mid + res)
                     total = res if total is None else total + res
                 tmp[0:128, :] = total
                 halves.append(tmp[pl.ds(0, 64, stride=2), :] + tmp[pl.ds(1, 64, stride=2), :])
@@ -448,6 +512,48 @@
         unsent.extend(near + far)
         return near, far
 
+    def send_margin(p):
+        pair = pl.ds(2 * p, 2)
+        c = copy(pot.at[pair, :, pl.ds(0, 32), :], margin.at[pair], gx, south)
+        c.start()
+        return c
+
+    group = lax.broadcasted_iota(jnp.int32, (8, 128), 1) // 32
+
+    def windows(p):
+        def step(x, carry):
+            columns = [
+                jnp.concatenate([pot[2 * p + t, x], margin[2 * p + t, x]], axis=0) for t in range(2)
+            ]
+            taken = dot_left(selt[...], jnp.concatenate(columns, axis=1))
+            for t in range(2):
+                for k in range(10):
+                    total = None
+                    for j in range(4):
+                        piece = taken[32 * k + 8 * j : 32 * k + 8 * j + 8, 128 * t : 128 * t + 128]
+                        piece = pltpu.roll(piece, lax.rem(128 + 32 * j - usual[k][1], 128), 1)
+                        total = piece if total is None else jnp.where(group == j, piece, total)
+                    if k < 2:
+                        wins[p][x, k, t] = total
+                    else:
+                        cut[p, k // 2 - 1, x, k % 2, t] = total
+            return carry
+
+        lax.fori_loop(0, 8, step, 0)
+
+    def give_back(p):
+        c, w = cut.at[p], wins[p]
+        pieces = [
+            (4, c.at[3], w.at[pl.ds(32, 8)]),
+            (3, c.at[2], w.at[pl.ds(24, 8)]),
+            (2, c.at[1, :, 0], w.at[pl.ds(16, 8), 0]),
+        ]
+        relays = [
+            (1, c.at[0], w.at[pl.ds(8, 8)], hold3.at[p], 3),
+            (2, c.at[1, :, 1], w.at[pl.ds(16, 8), 1], hold4.at[p], 2),
+        ]
+        return Shift(-1, pieces, relays, send, recv, slots(7))
+
     moves[0].arrive()
     accumulate(0)
     rims0 = send_rim(0)
@@ -455,12 +561,19 @@
     join_rim(0, rims0)
     down0(0)
     near0, far0 = swap(f1p.at[0], 4, 64)
+    edge0 = send_margin(0)
     moves[1].arrive()
     accumulate(1)
     rims1 = send_rim(1)
+    backs = [give_back(0), give_back(1)]
+    edge0.wait_recv()
+    windows(0)
     join_rim(1, rims1)
     down0(1)
     near1, far1 = swap(f1p.at[1], 4, 64)
+    edge1 = send_margin(1)
+    backs[0].start()
+    selc[...] = select_coarse(usual)
 
     def down1(p, xc):
         scale = DAMPING / center_of(1) / 4.0
@@ -484,6 +597,9 @@
     for xc in range(2):
         f2p[2 + xc, 8:40] = held[xc] + down1(1, xc)
     near2, far2 = swap(f2p, 2, 32)
+    edge1.wait_recv()
+    windows(1)
+    backs[1].start()
     for c in near2:
         c.wait_recv()
 
@@ -508,6 +624,8 @@
     for c in copies:
         c.start()
     unsent.extend(copies)
+    for k in range(10):
+        selz[k] = select_coarse_z(usual[k][1])
     mine = qs[gy]
     for d, c in enumerate(copies):
         c.wait_recv()
@@ -530,6 +648,9 @@
 
     lax.fori_loop(1, n, begin, 0)
     gall[gx] = mine
+    for b in range(2):
+        for j in range(4):
+            zp[b, 128 * j : 128 * j + 128], zs[b, 128 * j : 128 * j + 128] = widen_lanes(az_ref[b], j)
     lax.fori_loop(1, n, end, 0)
     spectrum = dot_high(kx_ref[...], gall[...].reshape(8 * n, 128)) * inv_ref[gy]
     for s, x in enumerate((west, gx, east)):
@@ -543,6 +664,7 @@
         c.start()
     unsent.extend(copies)
     ur[gy] = us[...]
+    backs[0].pass_on()
     for c in copies:
         c.wait_recv()
 
@@ -579,7 +701,7 @@
             mid = v1p[e]
             beside = v1p[e - 1] + v1p[e + 1] + pltpu.roll(mid, 1, 0) + pltpu.roll(mid, 79, 0)
             beside = beside + z_beside(mid, 64)
-            w1[e - 1] = (1.0 - DAMPING) * mid + scale * f1p[p, e] + (scale / 4.0) * beside
+            w1[p, e - 1] = (1.0 - DAMPING) * mid + scale * f1p[p, e] + (scale / 4.0) * beside
             return carry
 
         lax.fori_loop(1, 7, step, 0)
@@ -587,82 +709,82 @@
     def rise0(p):
         scale = DAMPING / center_of(0)
 
-        def widen(i):
-            wide = dot_right(w1[i, 4:76], p0_ref[...])
+        def widen(i, planes):
+            wide = dot_right(w1[p, i, 4:76], p0_ref[...])
             for t in range(2):
-                tmp1[t, pl.ds(0, 72, stride=2), :] = wide[:, 128 * t : 128 * t + 128]
-                tmp1[t, pl.ds(1, 72, stride=2), :] = wide[:, 128 * t : 128 * t + 128]
-
-        for i, e in ((0, 0), (5, 9)):
-            widen(i)
-            for t in range(2):
-                v0[e, t] = scale * fp[e, 2 * p + t] + tmp1[t]
+                value = wide[:, 128 * t : 128 * t + 128]
+                for e in planes:
+                    v0[e, t, pl.ds(0, 72, stride=2), :] = value
+                    v0[e, t, pl.ds(1, 72, stride=2), :] = value
+
+        widen(0, (0,))
 
         def lift(i, carry):
-            widen(i)
-            for x in range(2):
-                for t in range(2):
-                    v0[2 * i - 1 + x, t] = scale * fp[2 * i - 1 + x, 2 * p + t] + tmp1[t]
+            widen(i, (2 * i - 1, 2 * i))
             return carry
 
         lax.fori_loop(1, 5, lift, 0)
+        widen(5, (9,))
 
         def step(e, carry):
             for t in range(2):
                 mid = v0[e, t, 8:136]
                 beside = v0[e, t, 7:135] + v0[e, t, 9:137] + v0[e - 1, t, 8:136] + v0[e + 1, t, 8:136]
                 beside = beside + z_beside(mid, 128)
-                pot[2 * p + t, e - 1] = (1.0 - DAMPING) * mid + scale * (fp[e, 2 * p + t, 8:136] + beside)
+                pot[2 * p + t, e - 1] = pot[2 * p + t, e - 1] + (1.0 - DAMPING) * mid + scale * beside
             return carry
 
         lax.fori_loop(1, 9, step, 0)
-
-    def send_margin(p):
         pair = pl.ds(2 * p, 2)
-        c = copy(pot.at[pair, :, pl.ds(0, 32), :], margin.at[pair], gx, south)
-        c.start()
-        unsent.append(c)
         keep = pltpu.make_async_copy(pot.at[pair], out_ref.at[pair], local.at[1 + p])
         keep.start()
-        return c, keep
-
-    group = lax.broadcasted_iota(jnp.int32, (8, 128), 1) // 32
-
-    def windows(p):
-        def step(x, carry):
-            columns = [
-                jnp.concatenate([pot[2 * p + t, x], margin[2 * p + t, x]], axis=0) for t in range(2)
-            ]
-            taken = dot_left(selt[...], jnp.concatenate(columns, axis=1))
-            for t in range(2):
-                for k in range(10):
-                    total = None
-                    for j in range(4):
-                        piece = taken[32 * k + 8 * j : 32 * k + 8 * j + 8, 128 * t : 128 * t + 128]
-                        piece = pltpu.roll(piece, lax.rem(128 + 32 * j - usual[k][1], 128), 1)
-                        total = piece if total is None else jnp.where(group == j, piece, total)
-                    if k < 2:
-                        wins[p][x, k, t] = total
-                    else:
-                        cut[p, k // 2 - 1, x, k % 2, t] = total
-            return carry
-
-        lax.fori_loop(0, 8, step, 0)
-
-    def give_back(p):
-        c, w = cut.at[p], wins[p]
+        return keep
+
+    def windows1():
+        for i in range(5):
+            columns = [jnp.concatenate([w1[p, i, 0:72], mar1[p, i]], axis=0) for p in range(2)]
+            hi, lo = split2(jnp.concatenate(columns, axis=1))
+            taken[2 * i] = dot(selc[...], hi).astype(BF16)
+            taken[2 * i + 1] = dot(selc[...], lo).astype(BF16)
+        for k in range(10):
+            rows = jnp.concatenate([taken[i, 32 * k : 32 * k + 32] for i in range(10)], axis=0)
+            rows = dot(rows, selz[k])
+            for i in range(5):
+                part = rows[64 * i : 64 * i + 24] + rows[64 * i + 32 : 64 * i + 56]
+                if k < 2:
+                    cwin[i, k] = part
+                elif i > 0:
+                    cut1[k // 2 - 1, i - 1, k % 2] = part
+
+    def give_back1():
         pieces = [
-            (4, c.at[3], w.at[pl.ds(32, 8)]),
-            (3, c.at[2], w.at[pl.ds(24, 8)]),
-            (2, c.at[1, :, 0], w.at[pl.ds(16, 8), 0]),
+            (4, cut1.at[3], cwin.at[pl.ds(17, 4)]),
+            (3, cut1.at[2], cwin.at[pl.ds(13, 4)]),
+            (2, cut1.at[1, :, 0], cwin.at[pl.ds(9, 4), 0]),
         ]
         relays = [
-            (1, c.at[0], w.at[pl.ds(8, 8)], hold3.at[p], 3),
-            (2, c.at[1, :, 1], w.at[pl.ds(16, 8), 1], hold4.at[p], 2),
+            (1, cut1.at[0], cwin.at[pl.ds(5, 4)], hold5, 3),
+            (2, cut1.at[1, :, 1], cwin.at[pl.ds(9, 4), 1], hold6, 2),
         ]
         return Shift(-1, pieces, relays, send, recv, slots(7))
 
-    def project(p):
+    def expand(b):
+        rows = widen_rows(ay_ref[b])
+        blank = jnp.zeros((8, 128), F32)
+        for g in range(11):
+            planes = [x for x in (2 * g, 2 * g + 1) if x < 21]
+            columns = [jnp.concatenate([cwin[x, b], blank], axis=0) for x in planes]
+            wide = dot_left(rows, jnp.concatenate(columns, axis=1))
+            for i, x in enumerate(planes):
+                for j in range(4):
+                    here = wide[:, 128 * i : 128 * i + 128]
+                    lc1[8 * x : 8 * x + 8, 128 * j : 128 * j + 128] = here[8 * j : 8 * j + 8]
+                    lc2[8 * x : 8 * x + 8, 128 * j : 128 * j + 128] = here[32 + 8 * j : 40 + 8 * j]
+        ub[b] = dot_right(lc1[...], zp[b]).reshape(21, 8, 512)
+        vb[b] = (dot_right(lc2[...], zp[b]) + dot_right(lc1[...], zs[b])).reshape(21, 8, 512)
+
+    def project():
+        scale = DAMPING / center_of(0)
         for b in range(2):
 
             def step(s, total, b=b):
@@ -672,53 +794,63 @@
                     occ = occ_ref[b, :, rows, :].astype(F32)
                     vir = vir_ref[b, :, rows, :].astype(F32)
                     for g in range(2):
-                        cells = wins[p][ax_ref[b] + s * 8 + 2 * h + g, b]
-                        weighted = occ[None, :, 8 * g : 8 * g + 8] * cells[:, None]
-                        left.append(weighted.reshape(128, 128).astype(BF16))
+                        x = ax_ref[b] + s * 8 + 2 * h + g
+                        mid = ub[b, halve(x + 2)]
+                        late = (1.0 - DAMPING) * mid
+                        late = late + scale * (ub[b, halve(x + 1)] + ub[b, halve(x + 3)] + vb[b, halve(x + 2)])
+                        parts = []
+                        for t in range(4):
+                            cells = wins[t // 2][x, b, t % 2] + late[:, 128 * t : 128 * t + 128]
+                            weighted = occ[:, 8 * g : 8 * g + 8] * cells[None]
+                            parts.append(weighted.reshape(64, 128).astype(BF16))
+                        left.append(jnp.concatenate(parts, axis=0))
                         right.append(vir[:, 8 * g : 8 * g + 8].reshape(64, 128).astype(BF16))
                 left, right = jnp.concatenate(left, axis=1), jnp.concatenate(right, axis=1)
                 return total + lax.dot_general(
                     left, right, (((1,), (1,)), ((), ())), preferred_element_type=F32
                 )
 
-            total = lax.fori_loop(0, 4, step, jnp.zeros((128, 64), F32))
-            row = lax.broadcasted_iota(jnp.int32, (128, 64), 0) % 8
-            col = lax.broadcasted_iota(jnp.int32, (128, 64), 1) % 8
+            total = lax.fori_loop(0, 4, step, jnp.zeros((256, 64), F32))
+            row = lax.broadcasted_iota(jnp.int32, (256, 64), 0) % 8
+            col = lax.broadcasted_iota(jnp.int32, (256, 64), 1) % 8
             total = jnp.where(row == col, total, 0.0)
-            total = jnp.sum(total.reshape(16, 8, 64), axis=1)
+            total = jnp.sum(total.reshape(32, 8, 64), axis=1)
             col = lax.broadcasted_iota(jnp.int32, (64, 128), 1)
             row = lax.broadcasted_iota(jnp.int32, (64, 128), 0) // 8
             pick = jnp.where(row == col, float(BOX) ** (-1.5), 0.0)
-            coup_ref[b, 16 * p : 16 * p + 16] = dot_high(total, pick)
+            coup_ref[b] = dot_high(total, pick)
 
     for c in far0:
         c.wait_recv()
     rise1(0)
-    rise0(0)
-    edge0, keep0 = send_margin(0)
     for c in far1:
         c.wait_recv()
     rise1(1)
-    rise0(1)
-    edge1, keep1 = send_margin(1)
-    backs = [give_back(0), give_back(1)]
-    edge0.wait_recv()
-    windows(0)
-    backs[0].start()
-    edge1.wait_recv()
-    windows(1)
-    backs[1].start()
-    backs[0].pass_on()
+    margins = [copy(w1.at[p, pl.ds(0, 5), pl.ds(8, 24)], mar1.at[p], gx, south) for p in range(2)]
+    for c in margins:
+        c.start()
+    edge0.wait_send()
+    edge1.wait_send()
+    backs[1].pass_on()
+    keeps = [rise0(0)]
+    for c in margins:
+        c.wait_recv()
+    windows1()
+    late = give_back1()
+    late.start()
+    keeps.append(rise0(1))
+    late.pass_on()
     backs[0].arrive()
-    backs[1].pass_on()
-    project(0)
     backs[1].arrive()
-    project(1)
-    keep0.wait()
-    keep1.wait()
-    for c in unsent:
+    late.arrive()
+    expand(0)
+    expand(1)
+    project()
+    for c in keeps:
+        c.wait()
+    for c in unsent + margins:
         c.wait_send()
-    for c in moves + backs:
+    for c in moves + backs + [late]:
         c.settle()
 
 
@@ -733,17 +865,13 @@
 def per_device(slabs, tiles, occupied, virtual, trials, anchor_x, anchor_y, anchor_z):
     occ = occupied.reshape(2, 8, 256, 128)
     vir = virtual.reshape(2, 8, 256, 128)
-    mix = jnp.einsum("bpsia,mn->bpisman", trials.reshape(2, 2, 2, 8, 8), jnp.eye(8, dtype=BF16))
-    mix = mix.reshape(2, 2, 128, 64)
-    anchors = jnp.concatenate([anchor_y, anchor_z, jnp.zeros((124,), jnp.int32)])
-    anchors = jnp.broadcast_to(anchors[None], (8, 128))
     tab = tables(slabs, tiles)
     exact = [jnp.asarray(tab[k], BF16) for k in ("r0", "r1", "p1", "p0")]
     wide = [jnp.asarray(tab[k], F32) for k in ("fz", "bz", "fy", "by", "kx", "inv")]
     potential, coupling = pl.pallas_call(
         whole_kernel,
         out_shape=(shaped((4, 8, 128, 128)), shaped((2, 32, 128))),
-        in_specs=[SMEM, SMEM] + [VMEM] * 14,
+        in_specs=[SMEM] * 3 + [VMEM] * 13,
         out_specs=(ANY, VMEM),
         scratch_shapes=[
             pltpu.VMEM((2, 48, 2, 8, 128), F32),
@@ -764,11 +892,10 @@
             pltpu.VMEM((6, 48, 128), F32),
             pltpu.VMEM((10, 2, 144, 128), F32),
             pltpu.VMEM((8, 80, 128), F32),
-            pltpu.VMEM((6, 80, 128), F32),
+            pltpu.VMEM((2, 6, 80, 128), F32),
             pltpu.VMEM((6, 48, 128), F32),
             pltpu.VMEM((4, 48, 128), F32),
             pltpu.VMEM((144, 128), F32),
-            pltpu.VMEM((2, 144, 128), F32),
             pltpu.VMEM((tiles, 8, 128), F32),
             pltpu.VMEM((tiles, 8, 128), F32),
             pltpu.VMEM((8, 128), F32),
@@ -782,6 +909,21 @@
             pltpu.VMEM((40, 2, 2, 8, 128), F32),
             pltpu.VMEM((2, 8, 2, 2, 8, 128), F32),
             pltpu.VMEM((2, 8, 2, 8, 128), F32),
+            pltpu.VMEM((8, 128), jnp.int32),
+            pltpu.VMEM((2, 5, 24, 128), F32),
+            pltpu.VMEM((320, 96), BF16),
+            pltpu.VMEM((10, 256, 128), BF16),
+            pltpu.VMEM((10, 320, 256), BF16),
+            pltpu.VMEM((4, 4, 2, 24, 128), F32),
+            pltpu.VMEM((21, 2, 24, 128), F32),
+            pltpu.VMEM((4, 2, 24, 128), F32),
+            pltpu.VMEM((4, 24, 128), F32),
+            pltpu.VMEM((168, 512), F32),
+            pltpu.VMEM((168, 512), F32),
+            pltpu.VMEM((2, 512, 512), BF16),
+            pltpu.VMEM((2, 512, 512), BF16),
+            pltpu.VMEM((2, 21, 8, 512), F32),
+            pltpu.VMEM((2, 21, 8, 512), F32),
             pltpu.SemaphoreType.DMA((96,)),
             pltpu.SemaphoreType.DMA((96,)),
             pltpu.SemaphoreType.DMA((slabs,)),
@@ -790,7 +932,7 @@
         ],
         compiler_params=params(collective_id=0, has_side_effects=True),
         name="whole",
-    )(anchor_x, anchors, anchors, occ, vir, mix, *exact, *wide)
+    )(anchor_x, anchor_y, anchor_z, occ, vir, trials.reshape(2, 32, 8), *exact, *wide)
     return potential, coupling[:, :, :8].reshape(2, 4, 8, 8)
 
 

time: 118 us -> 110 us (0.932)
  the two profiles are of different devices: /device:TPU:13 before, /device:TPU:7 now
where the time goes in v4:
time: 110 us; the launch traced here: 109 us
  Pallas kernels  104 us (95%)
  local copies, waits for them, and re-layouts  4.13 us (4%)
    pallas_call x1, Pallas kernels, per_device(): pl.pallas_call(whole_kernel, out_shape=(shaped((4, 8, 128, 128)), shaped(...  104 us

profile of v4, /device:TPU:7, one launch (start us, length us, event | category | flops | bytes accessed | tf_op | source)
XLA Modules:
  0.0 109.2 jit_solution(3677682504364787142)
XLA Ops:
  0.6 0.0 copy-start
  0.6 0.0 copy-start.1
  0.7 0.0 copy-start.2
  0.7 0.0 copy-start.3
  0.7 0.0 copy-start.4
  0.7 0.0 copy-start.5
  0.7 0.0 copy-start.6
  0.7 0.0 copy-start.7
  0.7 0.0 copy-start.8
  0.7 0.0 copy-start.9
  0.8 0.0 copy-start.10
  0.8 0.0 copy-start.11
  0.8 0.0 copy-start.12
  0.8 0.0 copy-start.13
  0.8 2.1 %copy_bitcast_fusion = (bf16[2,8,256,128]{3,2,1,0:T(8,128)(2,1)S(1)}, bf16[2,8,256,128]{3,2,1,0:T(8,128)(2,1)S(1)}) fusion(bf16[2,8,256,128]{3,1,2,0:T(8,128)(2,1)} %bitcast.14, bf16[2,8,256,128]{3,1,2,0:T(8,128)(2,1)} %bitcast.15), kind=kLoop, calls=%fused_computation | loop fusion | bytes 4194304 | tf_op jit(solution)/shard_map/reshape | solution.py:867
  2.9 0.0 copy-done
  2.9 0.0 copy-done.1
  2.9 0.0 copy-done.2
  2.9 0.0 copy-done.3
  3.0 0.0 copy-done.4
  3.0 0.0 copy-done.5
  3.1 104.2 %whole.1 = (f32[4,8,128,128]{3,2,1,0:T(8,128)S(1)}, f32[2,32,128]{2,1,0:T(8,128)S(1)}) custom-call(s32[2]{0:T(128)S(1)} %copy-done.11, s32[2]{0:T(128)S(1)} %copy-done.12, s32[2]{0:T(128)S(1)} %copy-done.13, bf16[2,8,256,128]{3,2,1,0:T(8,128)(2,1)S(1)} %get-tuple-element.7.occ_ref, bf16[2,8,256,128]{3,2,1,0:T(8,128)(2,1)S(1)} %get-tuple-element.6.vir_ref, ...), custom_call_target="tpu_custom_call" | custom-call | tf_op jit(solution)/shard_map/whole/pallas_call | solution.py:871
  107.3 0.6 slice_bitcast_fusion
  107.9 1.3 %copy.23 = f32[4,8,128,128]{3,2,1,0:T(8,128)} copy(f32[4,8,128,128]{3,2,1,0:T(8,128)S(1)} %get-tuple-element.10) | data formatting | bytes 4194304
  (8 shorter events, 0.0 us)
Async XLA Ops:
  0.6 2.3 %copy-start = (f32[4,256,128]{2,1,0:T(8,128)S(1)}, f32[4,256,128]{2,1,0:T(8,128)}, u32[]{:S(2)}) copy-start(f32[4,256,128]{2,1,0:T(8,128)} %constant.29.clone.inv_ref) | copy-start | bytes 1572868
  0.6 2.3 %copy-start.1 = (f32[256,256]{1,0:T(8,128)S(1)}, f32[256,256]{1,0:T(8,128)}, u32[]{:S(2)}) copy-start(f32[256,256]{1,0:T(8,128)} %constant.28.clone.kx_ref) | copy-start | bytes 786436
  0.7 2.3 %copy-start.2 = (f32[4,64,128]{2,1,0:T(8,128)S(1)}, f32[4,64,128]{2,1,0:T(8,128)}, u32[]{:S(2)}) copy-start(f32[4,64,128]{2,1,0:T(8,128)} %constant.26.clone.fy_ref) | copy-start | bytes 393220
  0.7 2.3 %copy-start.3 = (f32[4,48,128]{2,1,0:T(8,128)S(1)}, f32[4,48,128]{2,1,0:T(8,128)}, u32[]{:S(2)}) copy-start(f32[4,48,128]{2,1,0:T(8,128)} %constant.27.clone.by_ref) | copy-start | bytes 294916
  0.7 2.3 %copy-start.4 = (f32[128,128]{1,0:T(8,128)S(1)}, f32[128,128]{1,0:T(8,128)}, u32[]{:S(2)}) copy-start(f32[128,128]{1,0:T(8,128)} %constant.25.clone.bz_ref) | copy-start | bytes 196612
  0.7 2.3 %copy-start.5 = (f32[128,128]{1,0:T(8,128)S(1)}, f32[128,128]{1,0:T(8,128)}, u32[]{:S(2)}) copy-start(f32[128,128]{1,0:T(8,128)} %constant.24.clone.fz_ref) | copy-start | bytes 196612
  0.7 2.3 %copy-start.6 = (bf16[128,256]{1,0:T(8,128)(2,1)S(1)}, bf16[128,256]{1,0:T(8,128)(2,1)}, u32[]{:S(2)}) copy-start(bf16[128,256]{1,0:T(8,128)(2,1)} %constant.23.clone.p0_ref) | copy-start | bytes 196612
  0.7 2.3 %copy-start.7 = (bf16[2,128,128]{2,1,0:T(8,128)(2,1)S(1)}, bf16[2,128,128]{2,1,0:T(8,128)(2,1)}, u32[]{:S(2)}) copy-start(bf16[2,128,128]{2,1,0:T(8,128)(2,1)} %constant.22.clone.p1_ref) | copy-start | bytes 196612
  0.7 2.3 %copy-start.8 = (bf16[2,128,128]{2,1,0:T(8,128)(2,1)S(1)}, bf16[2,128,128]{2,1,0:T(8,128)(2,1)}, u32[]{:S(2)}) copy-start(bf16[2,128,128]{2,1,0:T(8,128)(2,1)} %constant.21.clone.r1_ref) | copy-start | bytes 196612
  0.7 2.3 %copy-start.9 = (bf16[256,128]{1,0:T(8,128)(2,1)S(1)}, bf16[256,128]{1,0:T(8,128)(2,1)}, u32[]{:S(2)}) copy-start(bf16[256,128]{1,0:T(8,128)(2,1)} %constant.20.clone.r0_ref) | copy-start | bytes 196612
  0.8 2.3 %copy-start.10 = (bf16[2,4,8,8]{3,2,1,0:T(8,128)(2,1)S(1)}, bf16[2,4,8,8]{3,2,1,0:T(8,128)(2,1)}, u32[]{:S(2)}) copy-start(bf16[2,4,8,8]{3,2,1,0:T(8,128)(2,1)} %param.18) | copy-start | bytes 3076
  0.8 2.3 %copy-start.11 = (s32[2]{0:T(128)S(1)}, s32[2]{0:T(128)}, u32[]{:S(2)}) copy-start(s32[2]{0:T(128)} %ax_ref.1) | copy-start | bytes 28
  0.8 2.3 %copy-start.12 = (s32[2]{0:T(128)S(1)}, s32[2]{0:T(128)}, u32[]{:S(2)}) copy-start(s32[2]{0:T(128)} %ay_ref.1) | copy-start | bytes 28
  0.8 2.3 %copy-start.13 = (s32[2]{0:T(128)S(1)}, s32[2]{0:T(128)}, u32[]{:S(2)}) copy-start(s32[2]{0:T(128)} %az_ref.1) | copy-start | bytes 28

commit v5 on v4

--- a/solution.py
+++ b/solution.py
@@ -572,7 +572,6 @@
     down0(1)
     near1, far1 = swap(f1p.at[1], 4, 64)
     edge1 = send_margin(1)
-    backs[0].start()
     selc[...] = select_coarse(usual)
 
     def down1(p, xc):
@@ -597,9 +596,7 @@
     for xc in range(2):
         f2p[2 + xc, 8:40] = held[xc] + down1(1, xc)
     near2, far2 = swap(f2p, 2, 32)
-    edge1.wait_recv()
-    windows(1)
-    backs[1].start()
+    backs[0].start()
     for c in near2:
         c.wait_recv()
 
@@ -624,6 +621,9 @@
     for c in copies:
         c.start()
     unsent.extend(copies)
+    edge1.wait_recv()
+    windows(1)
+    backs[1].start()
     for k in range(10):
         selz[k] = select_coarse_z(usual[k][1])
     mine = qs[gy]

time: 110 us -> 109 us (level)
  no operation moved by 1% of the time
where the time goes in v5:
time: 109 us; the launch traced here: 108 us
  Pallas kernels  103 us (94%)
  local copies, waits for them, and re-layouts  4.13 us (4%)
    pallas_call x1, Pallas kernels, per_device(): pl.pallas_call(whole_kernel, out_shape=(shaped((4, 8, 128, 128)), shaped(...  103 us

profile of v5, /device:TPU:7, one launch (start us, length us, event | category | flops | bytes accessed | tf_op | source)
XLA Modules:
  0.0 108.5 jit_solution(937530824059649426)
XLA Ops:
  0.6 0.0 copy-start
  0.6 0.0 copy-start.1
  0.7 0.0 copy-start.2
  0.7 0.0 copy-start.3
  0.7 0.0 copy-start.4
  0.7 0.0 copy-start.5
  0.7 0.0 copy-start.6
  0.7 0.0 copy-start.7
  0.7 0.0 copy-start.8
  0.7 0.0 copy-start.9
  0.8 0.0 copy-start.10
  0.8 0.0 copy-start.11
  0.8 0.0 copy-start.12
  0.8 0.0 copy-start.13
  0.8 2.1 %copy_bitcast_fusion = (bf16[2,8,256,128]{3,2,1,0:T(8,128)(2,1)S(1)}, bf16[2,8,256,128]{3,2,1,0:T(8,128)(2,1)S(1)}) fusion(bf16[2,8,256,128]{3,1,2,0:T(8,128)(2,1)} %bitcast.14, bf16[2,8,256,128]{3,1,2,0:T(8,128)(2,1)} %bitcast.15), kind=kLoop, calls=%fused_computation | loop fusion | bytes 4194304 | tf_op jit(solution)/shard_map/reshape | solution.py:867
  2.9 0.0 copy-done
  2.9 0.0 copy-done.1
  2.9 0.0 copy-done.2
  2.9 0.0 copy-done.3
  3.0 0.0 copy-done.4
  3.0 0.0 copy-done.5
  3.1 103.5 %whole.1 = (f32[4,8,128,128]{3,2,1,0:T(8,128)S(1)}, f32[2,32,128]{2,1,0:T(8,128)S(1)}) custom-call(s32[2]{0:T(128)S(1)} %copy-done.11, s32[2]{0:T(128)S(1)} %copy-done.12, s32[2]{0:T(128)S(1)} %copy-done.13, bf16[2,8,256,128]{3,2,1,0:T(8,128)(2,1)S(1)} %get-tuple-element.7.occ_ref, bf16[2,8,256,128]{3,2,1,0:T(8,128)(2,1)S(1)} %get-tuple-element.6.vir_ref, ...), custom_call_target="tpu_custom_call" | custom-call | tf_op jit(solution)/shard_map/whole/pallas_call | solution.py:871
  106.5 0.6 slice_bitcast_fusion
  107.1 1.3 %copy.23 = f32[4,8,128,128]{3,2,1,0:T(8,128)} copy(f32[4,8,128,128]{3,2,1,0:T(8,128)S(1)} %get-tuple-element.10) | data formatting | bytes 4194304
  (8 shorter events, 0.0 us)
Async XLA Ops:
  0.6 2.3 %copy-start = (f32[4,256,128]{2,1,0:T(8,128)S(1)}, f32[4,256,128]{2,1,0:T(8,128)}, u32[]{:S(2)}) copy-start(f32[4,256,128]{2,1,0:T(8,128)} %constant.29.clone.inv_ref) | copy-start | bytes 1572868
  0.6 2.3 %copy-start.1 = (f32[256,256]{1,0:T(8,128)S(1)}, f32[256,256]{1,0:T(8,128)}, u32[]{:S(2)}) copy-start(f32[256,256]{1,0:T(8,128)} %constant.28.clone.kx_ref) | copy-start | bytes 786436
  0.7 2.3 %copy-start.2 = (f32[4,64,128]{2,1,0:T(8,128)S(1)}, f32[4,64,128]{2,1,0:T(8,128)}, u32[]{:S(2)}) copy-start(f32[4,64,128]{2,1,0:T(8,128)} %constant.26.clone.fy_ref) | copy-start | bytes 393220
  0.7 2.3 %copy-start.3 = (f32[4,48,128]{2,1,0:T(8,128)S(1)}, f32[4,48,128]{2,1,0:T(8,128)}, u32[]{:S(2)}) copy-start(f32[4,48,128]{2,1,0:T(8,128)} %constant.27.clone.by_ref) | copy-start | bytes 294916
  0.7 2.3 %copy-start.4 = (f32[128,128]{1,0:T(8,128)S(1)}, f32[128,128]{1,0:T(8,128)}, u32[]{:S(2)}) copy-start(f32[128,128]{1,0:T(8,128)} %constant.25.clone.bz_ref) | copy-start | bytes 196612
  0.7 2.3 %copy-start.5 = (f32[128,128]{1,0:T(8,128)S(1)}, f32[128,128]{1,0:T(8,128)}, u32[]{:S(2)}) copy-start(f32[128,128]{1,0:T(8,128)} %constant.24.clone.fz_ref) | copy-start | bytes 196612
  0.7 2.3 %copy-start.6 = (bf16[128,256]{1,0:T(8,128)(2,1)S(1)}, bf16[128,256]{1,0:T(8,128)(2,1)}, u32[]{:S(2)}) copy-start(bf16[128,256]{1,0:T(8,128)(2,1)} %constant.23.clone.p0_ref) | copy-start | bytes 196612
  0.7 2.3 %copy-start.7 = (bf16[2,128,128]{2,1,0:T(8,128)(2,1)S(1)}, bf16[2,128,128]{2,1,0:T(8,128)(2,1)}, u32[]{:S(2)}) copy-start(bf16[2,128,128]{2,1,0:T(8,128)(2,1)} %constant.22.clone.p1_ref) | copy-start | bytes 196612
  0.7 2.3 %copy-start.8 = (bf16[2,128,128]{2,1,0:T(8,128)(2,1)S(1)}, bf16[2,128,128]{2,1,0:T(8,128)(2,1)}, u32[]{:S(2)}) copy-start(bf16[2,128,128]{2,1,0:T(8,128)(2,1)} %constant.21.clone.r1_ref) | copy-start | bytes 196612
  0.7 2.3 %copy-start.9 = (bf16[256,128]{1,0:T(8,128)(2,1)S(1)}, bf16[256,128]{1,0:T(8,128)(2,1)}, u32[]{:S(2)}) copy-start(bf16[256,128]{1,0:T(8,128)(2,1)} %constant.20.clone.r0_ref) | copy-start | bytes 196612
  0.8 2.3 %copy-start.10 = (bf16[2,4,8,8]{3,2,1,0:T(8,128)(2,1)S(1)}, bf16[2,4,8,8]{3,2,1,0:T(8,128)(2,1)}, u32[]{:S(2)}) copy-start(bf16[2,4,8,8]{3,2,1,0:T(8,128)(2,1)} %param.18) | copy-start | bytes 3076
  0.8 2.3 %copy-start.11 = (s32[2]{0:T(128)S(1)}, s32[2]{0:T(128)}, u32[]{:S(2)}) copy-start(s32[2]{0:T(128)} %ax_ref.1) | copy-start | bytes 28
  0.8 2.3 %copy-start.12 = (s32[2]{0:T(128)S(1)}, s32[2]{0:T(128)}, u32[]{:S(2)}) copy-start(s32[2]{0:T(128)} %ay_ref.1) | copy-start | bytes 28
  0.8 2.3 %copy-start.13 = (s32[2]{0:T(128)S(1)}, s32[2]{0:T(128)}, u32[]{:S(2)}) copy-start(s32[2]{0:T(128)} %az_ref.1) | copy-start | bytes 28

commit v6 on v5

--- a/solution.py
+++ b/solution.py
@@ -832,14 +832,14 @@
     edge0.wait_send()
     edge1.wait_send()
     backs[1].pass_on()
-    keeps = [rise0(0)]
     for c in margins:
         c.wait_recv()
     windows1()
     late = give_back1()
     late.start()
+    keeps = [rise0(0)]
+    late.pass_on()
     keeps.append(rise0(1))
-    late.pass_on()
     backs[0].arrive()
     backs[1].arrive()
     late.arrive()

time: 109 us -> 109 us (level)
  no operation moved by 1% of the time
where the time goes in v6:
time: 109 us; the launch traced here: 108 us
  Pallas kernels  103 us (94%)
  local copies, waits for them, and re-layouts  4.13 us (4%)
    pallas_call x1, Pallas kernels, per_device(): pl.pallas_call(whole_kernel, out_shape=(shaped((4, 8, 128, 128)), shaped(...  103 us

profile of v6, /device:TPU:7, one launch (start us, length us, event | category | flops | bytes accessed | tf_op | source)
XLA Modules:
  0.0 107.7 jit_solution(485220879198045125)
XLA Ops:
  0.6 0.0 copy-start
  0.6 0.0 copy-start.1
  0.7 0.0 copy-start.2
  0.7 0.0 copy-start.3
  0.7 0.0 copy-start.4
  0.7 0.0 copy-start.5
  0.7 0.0 copy-start.6
  0.7 0.0 copy-start.7
  0.7 0.0 copy-start.8
  0.7 0.0 copy-start.9
  0.8 2.1 %copy_bitcast_fusion = (bf16[2,8,256,128]{3,2,1,0:T(8,128)(2,1)S(1)}, bf16[2,8,256,128]{3,2,1,0:T(8,128)(2,1)S(1)}) fusion(bf16[2,8,256,128]{3,1,2,0:T(8,128)(2,1)} %bitcast.14, bf16[2,8,256,128]{3,1,2,0:T(8,128)(2,1)} %bitcast.15), kind=kLoop, calls=%fused_computation | loop fusion | bytes 4194304 | tf_op jit(solution)/shard_map/reshape | solution.py:867
  2.9 0.0 copy-done
  2.9 0.0 copy-done.1
  2.9 0.0 copy-done.2
  2.9 0.0 copy-done.3
  3.0 0.0 copy-done.4
  3.0 0.0 copy-done.5
  3.0 0.0 copy-done.6
  3.0 0.0 copy-done.7
  3.0 0.0 copy-done.8
  3.0 0.0 copy-done.9
  3.1 102.7 %whole.1 = (f32[4,8,128,128]{3,2,1,0:T(8,128)S(1)}, f32[2,32,128]{2,1,0:T(8,128)S(1)}) custom-call(s32[2]{0:T(128)S(1)} %copy-done.11, s32[2]{0:T(128)S(1)} %copy-done.12, s32[2]{0:T(128)S(1)} %copy-done.13, bf16[2,8,256,128]{3,2,1,0:T(8,128)(2,1)S(1)} %get-tuple-element.7.occ_ref, bf16[2,8,256,128]{3,2,1,0:T(8,128)(2,1)S(1)} %get-tuple-element.6.vir_ref, ...), custom_call_target="tpu_custom_call" | custom-call | tf_op jit(solution)/shard_map/whole/pallas_call | solution.py:871
  105.7 0.6 slice_bitcast_fusion
  106.3 1.3 %copy.23 = f32[4,8,128,128]{3,2,1,0:T(8,128)} copy(f32[4,8,128,128]{3,2,1,0:T(8,128)S(1)} %get-tuple-element.10) | data formatting | bytes 4194304
  (8 shorter events, 0.0 us)
Async XLA Ops:
  0.6 2.3 %copy-start = (f32[4,256,128]{2,1,0:T(8,128)S(1)}, f32[4,256,128]{2,1,0:T(8,128)}, u32[]{:S(2)}) copy-start(f32[4,256,128]{2,1,0:T(8,128)} %constant.29.clone.inv_ref) | copy-start | bytes 1572868
  0.6 2.3 %copy-start.1 = (f32[256,256]{1,0:T(8,128)S(1)}, f32[256,256]{1,0:T(8,128)}, u32[]{:S(2)}) copy-start(f32[256,256]{1,0:T(8,128)} %constant.28.clone.kx_ref) | copy-start | bytes 786436
  0.7 2.3 %copy-start.2 = (f32[4,64,128]{2,1,0:T(8,128)S(1)}, f32[4,64,128]{2,1,0:T(8,128)}, u32[]{:S(2)}) copy-start(f32[4,64,128]{2,1,0:T(8,128)} %constant.26.clone.fy_ref) | copy-start | bytes 393220
  0.7 2.3 %copy-start.3 = (f32[4,48,128]{2,1,0:T(8,128)S(1)}, f32[4,48,128]{2,1,0:T(8,128)}, u32[]{:S(2)}) copy-start(f32[4,48,128]{2,1,0:T(8,128)} %constant.27.clone.by_ref) | copy-start | bytes 294916
  0.7 2.3 %copy-start.4 = (f32[128,128]{1,0:T(8,128)S(1)}, f32[128,128]{1,0:T(8,128)}, u32[]{:S(2)}) copy-start(f32[128,128]{1,0:T(8,128)} %constant.25.clone.bz_ref) | copy-start | bytes 196612
  0.7 2.3 %copy-start.5 = (f32[128,128]{1,0:T(8,128)S(1)}, f32[128,128]{1,0:T(8,128)}, u32[]{:S(2)}) copy-start(f32[128,128]{1,0:T(8,128)} %constant.24.clone.fz_ref) | copy-start | bytes 196612
  0.7 2.3 %copy-start.6 = (bf16[128,256]{1,0:T(8,128)(2,1)S(1)}, bf16[128,256]{1,0:T(8,128)(2,1)}, u32[]{:S(2)}) copy-start(bf16[128,256]{1,0:T(8,128)(2,1)} %constant.23.clone.p0_ref) | copy-start | bytes 196612
  0.7 2.3 %copy-start.7 = (bf16[2,128,128]{2,1,0:T(8,128)(2,1)S(1)}, bf16[2,128,128]{2,1,0:T(8,128)(2,1)}, u32[]{:S(2)}) copy-start(bf16[2,128,128]{2,1,0:T(8,128)(2,1)} %constant.22.clone.p1_ref) | copy-start | bytes 196612
  0.7 2.3 %copy-start.8 = (bf16[2,128,128]{2,1,0:T(8,128)(2,1)S(1)}, bf16[2,128,128]{2,1,0:T(8,128)(2,1)}, u32[]{:S(2)}) copy-start(bf16[2,128,128]{2,1,0:T(8,128)(2,1)} %constant.21.clone.r1_ref) | copy-start | bytes 196612
  0.7 2.3 %copy-start.9 = (bf16[256,128]{1,0:T(8,128)(2,1)S(1)}, bf16[256,128]{1,0:T(8,128)(2,1)}, u32[]{:S(2)}) copy-start(bf16[256,128]{1,0:T(8,128)(2,1)} %constant.20.clone.r0_ref) | copy-start | bytes 196612
  0.8 2.3 %copy-start.10 = (bf16[2,4,8,8]{3,2,1,0:T(8,128)(2,1)S(1)}, bf16[2,4,8,8]{3,2,1,0:T(8,128)(2,1)}, u32[]{:S(2)}) copy-start(bf16[2,4,8,8]{3,2,1,0:T(8,128)(2,1)} %param.18) | copy-start | bytes 3076
  0.8 2.3 %copy-start.11 = (s32[2]{0:T(128)S(1)}, s32[2]{0:T(128)}, u32[]{:S(2)}) copy-start(s32[2]{0:T(128)} %ax_ref.1) | copy-start | bytes 28
  0.8 2.3 %copy-start.12 = (s32[2]{0:T(128)S(1)}, s32[2]{0:T(128)}, u32[]{:S(2)}) copy-start(s32[2]{0:T(128)} %ay_ref.1) | copy-start | bytes 28
  0.8 2.3 %copy-start.13 = (s32[2]{0:T(128)S(1)}, s32[2]{0:T(128)}, u32[]{:S(2)}) copy-start(s32[2]{0:T(128)} %az_ref.1) | copy-start | bytes 28
